TPU v7x, 512 devices: a whole 4x8x8 slice. The times are simulated.
512 devices in a mesh: seq: 64 (over z, y), ch: 8 (over x, core).
Axes of the slice: x: 4, y: 8, z: 8, core: 2. Of those that a mesh axis runs over, the one named last changes fastest.
Arguments:
- token_ids: int32 [32768], P('seq'), may hold values from 0 to 511
- embed_table: bfloat16 [512, 4096], P(None, 'ch')
- norm_gain: float32 [4096], P('ch'), may hold values from 0.5 to 1.5
- short_filters: float32 [2, 3, 7, 4096], P(None, None, None, 'ch')
- medium_filter: float32 [128, 4096], P(None, 'ch'), may hold values from -0.5 to 0.5
- mode_rates: float32 [16, 4096], P(None, 'ch'), as said below
- mode_residues: float32 [16, 4096], P(None, 'ch'), may hold values from -1.5 to 1.5
Outputs:
- result: bfloat16 [32768, 4096], P('seq', 'ch')
Inputs may be any that keep to these rules, and one draw needn't show every extreme that they name: `mode_rates`: positive decay rates.
All inputs are finite; a program needn't handle non-finite values.
Results may differ from a plain program's by a relative error of at most 0.012.
The roundings to bfloat16 on the way count: a program that leaves them out, or rounds other values in their place, can miss the bound.
Values may be sent and summed in bfloat16 or wider, within the bound.
No kernel may reach another device: no remote copies, remote signals or barrier semaphores. Data moves between devices by JAX's collectives and lax.ppermute only.
A program may use at most 64 MiB of HBM per device.

v0:
```python
import jax
import jax.numpy as jnp
from jax import lax
from jax.sharding import PartitionSpec as P


def passed_along(array, axis, by):
    length = lax.axis_size(axis)
    pairs = [(i, i + by) for i in range(length) if 0 <= i + by < length]
    return lax.ppermute(array, axis, pairs)


def depthwise(extended, kernel):
    return lax.conv_general_dilated(
        extended,
        jnp.flip(kernel, 0)[:, None, :],
        (1,),
        "VALID",
        dimension_numbers=("NWC", "WIO", "NWC"),
        feature_group_count=kernel.shape[1],
        precision=lax.Precision.HIGHEST,
    )


def causal_taps(extended, kernel):
    return depthwise(extended[None], kernel)[0]


def rounded(values):
    stored = values.astype(jnp.bfloat16)
    stored = lax.optimization_barrier(stored)
    return stored.astype(jnp.float32)


def link_states(earlier, later):
    return (earlier[0] * later[0], later[0] * earlier[1] + later[1])


def local(
    token_ids, embed_table, norm_gain, short_filters, medium_filter, mode_rates, mode_residues
):
    row_count = token_ids.shape[0]
    local_width = embed_table.shape[1]
    short_span = short_filters.shape[2] - 1
    medium_span = medium_filter.shape[0] - 1
    onehot_rows = (
        token_ids[:, None] == jnp.arange(embed_table.shape[0], dtype=jnp.int32)[None, :]
    ).astype(jnp.bfloat16)
    embedded = jnp.dot(onehot_rows, embed_table, preferred_element_type=jnp.float32)
    squares = lax.psum(jnp.sum(embedded * embedded, axis=1), "ch")
    inverse = lax.rsqrt(squares / (local_width * lax.axis_size("ch")) + 1e-06)
    normed = (embedded * inverse[:, None] * norm_gain[None, :]).astype(jnp.bfloat16)
    before = passed_along(normed[row_count - short_span :], "seq", 1)
    extended = jnp.concatenate([before, normed], 0).astype(jnp.float32)
    query_one = causal_taps(extended, short_filters[0, 0])
    gated = (
        causal_taps(extended, short_filters[0, 1]) * causal_taps(extended, short_filters[0, 2])
    ).astype(jnp.bfloat16)
    gated_before = passed_along(gated[row_count - medium_span :], "seq", 1)
    gated_long = jnp.concatenate([gated_before, gated], 0).astype(jnp.float32)
    middle = causal_taps(gated_long, medium_filter)
    first_out = (query_one * middle).astype(jnp.bfloat16)
    second_before = passed_along(first_out[row_count - short_span :], "seq", 1)
    second_ext = jnp.concatenate([second_before, first_out], 0).astype(jnp.float32)
    query_two = causal_taps(second_ext, short_filters[1, 0])
    driven = rounded(
        causal_taps(second_ext, short_filters[1, 1]) * causal_taps(second_ext, short_filters[1, 2])
    )
    block_rows = 128
    block_count = row_count // block_rows
    offsets = jnp.arange(block_rows, dtype=jnp.float32)
    powers = jnp.exp(-mode_rates[None] * offsets[:, None, None])
    coefficient = mode_residues * jnp.sqrt(-jnp.expm1(-2.0 * mode_rates))
    weights = powers * (jnp.exp(-mode_rates) * coefficient)[None]
    kernel_long = jnp.sum(powers * coefficient[None], axis=1)
    blocks = driven.reshape(block_count, block_rows, local_width)
    padded = jnp.pad(blocks, ((0, 0), (block_rows - 1, 0), (0, 0)))
    inside = depthwise(padded, kernel_long)
    endings = jnp.einsum(
        "jrc,njc->nrc", jnp.flip(powers, 0), blocks, precision=lax.Precision.HIGHEST
    )
    decays = jnp.broadcast_to(jnp.exp(-mode_rates * block_rows)[None], endings.shape)
    running = lax.associative_scan(link_states, (decays, endings), axis=0)
    starts = jnp.concatenate([jnp.zeros_like(endings[:1]), running[1][:-1]], 0)
    local_long = inside + jnp.einsum(
        "jrc,nrc->njc", weights, starts, precision=lax.Precision.HIGHEST
    )
    device_decay = jnp.exp(-mode_rates * row_count)
    device_state = running[1][-1]

    def advance(counter, incoming_state):
        return passed_along(device_decay * incoming_state + device_state, "seq", 1)

    incoming = lax.fori_loop(0, lax.axis_size("seq") - 1, advance, jnp.zeros_like(device_state))
    block_starts = jnp.arange(block_count, dtype=jnp.float32) * block_rows
    lifted = jnp.exp(-mode_rates[None] * block_starts[:, None, None]) * incoming[None]
    whole = local_long + jnp.einsum(
        "jrc,nrc->njc", weights, lifted, precision=lax.Precision.HIGHEST
    )
    return (query_two * whole.reshape(row_count, local_width)).astype(jnp.bfloat16)


def solution(mesh):
    placed = (
        P("seq"),
        P(None, "ch"),
        P("ch"),
        P(None, None, None, "ch"),
        P(None, "ch"),
        P(None, "ch"),
        P(None, "ch"),
    )
    return jax.shard_map(
        local, mesh=mesh, in_specs=placed, out_specs=P("seq", "ch"), check_vma=False
    )
```

profile of v0, /device:TPU:256, one launch (start us, length us, event | category | flops | bytes accessed | tf_op | source)
XLA Modules:
  0.0 685.2 jit_solution(1284891604029073820)
XLA Ops:
  2.3 14.7 %psum.7 = f32[512]{0:T(512)S(1)} all-reduce(f32[512]{0:T(512)S(1)} %get-tuple-element.73), channel_id=1, replica_groups=mesh['seq'=64,'ch'=8] {'ch'}, use_global_device_ids=true, to_apply=%region_1.0 | all-reduce | flops 512 | bytes 4096 | tf_op jit(solution)/shard_map/psum | solution.py:50
  42.2 11.6 %fusion.20 = bf16[1,512,512]{2,0,1:T(2,128)(2,1)S(1)} fusion(bf16[1,639,512]{2,1,0:T(8,128)(2,1)S(1)} %maximum_bitcast_fusion, f32[1,520,512]{2,0,1:T(1,128)S(1)} %copy-done.1, f32[128,1,512]{2,0,1:T(8,128)S(1)} %bitcast.80), kind=kOutput, calls=%fused_computation.29 | convolution fusion | flops 403177472 | bytes 2489344 | tf_op jit(solution)/shard_map/conv_general_dilated | solution.py:14
  56.7 7.2 %rev.38 = f32[128,16,512]{0,1,2:T(8,128)} reverse(f32[128,16,512]{0,1,2:T(8,128)} %get-tuple-element.58), dimensions={0} | reverse | bytes 8388608 | tf_op jit(solution)/shard_map/jit(_flip)/rev | solution.py:80
  83.3 577.0 %while.10 = (s32[]{:T(128)}, f32[16,512]{1,0:T(8,128)S(1)}, f32[16,512]{1,0:T(8,128)S(1)}, f32[16,512]{1,0:T(8,128)S(1)}, s32[]{:T(128)}) while((s32[]{:T(128)}, f32[16,512]{1,0:T(8,128)S(1)}, f32[16,512]{1,0:T(8,128)S(1)}, f32[16,512]{1,0:T(8,128)S(1)}, s32[]{:T(128)}) %tuple.39), condition=%wide.region_4.5_spmd, body=%wide.region_3.4_spmd.sunk | while | flops 16386 | bytes 262245 | solution.py:94
  94.4 7.2 %collective-permute-done = f32[16,512]{1,0:T(8,128)S(1)} collective-permute-done((f32[16,512]{1,0:T(8,128)S(1)}, f32[16,512]{1,0:T(8,128)S(1)}, u32[]{:S(2)}, u32[]{:S(2)}) %collective-permute-start) | collective-permute-done | bytes 32800 | tf_op jit(solution)/shard_map/while/body/eval_jaxpr/ppermute | solution.py:10
  103.6 7.2 %collective-permute-done = f32[16,512]{1,0:T(8,128)S(1)} collective-permute-done((f32[16,512]{1,0:T(8,128)S(1)}, f32[16,512]{1,0:T(8,128)S(1)}, u32[]{:S(2)}, u32[]{:S(2)}) %collective-permute-start) | collective-permute-done | bytes 32800 | tf_op jit(solution)/shard_map/while/body/eval_jaxpr/ppermute | solution.py:10
  112.7 7.4 %collective-permute-done = f32[16,512]{1,0:T(8,128)S(1)} collective-permute-done((f32[16,512]{1,0:T(8,128)S(1)}, f32[16,512]{1,0:T(8,128)S(1)}, u32[]{:S(2)}, u32[]{:S(2)}) %collective-permute-start) | collective-permute-done | bytes 32800 | tf_op jit(solution)/shard_map/while/body/eval_jaxpr/ppermute | solution.py:10
  122.1 7.2 %collective-permute-done = f32[16,512]{1,0:T(8,128)S(1)} collective-permute-done((f32[16,512]{1,0:T(8,128)S(1)}, f32[16,512]{1,0:T(8,128)S(1)}, u32[]{:S(2)}, u32[]{:S(2)}) %collective-permute-start) | collective-permute-done | bytes 32800 | tf_op jit(solution)/shard_map/while/body/eval_jaxpr/ppermute | solution.py:10
  131.2 7.2 %collective-permute-done = f32[16,512]{1,0:T(8,128)S(1)} collective-permute-done((f32[16,512]{1,0:T(8,128)S(1)}, f32[16,512]{1,0:T(8,128)S(1)}, u32[]{:S(2)}, u32[]{:S(2)}) %collective-permute-start) | collective-permute-done | bytes 32800 | tf_op jit(solution)/shard_map/while/body/eval_jaxpr/ppermute | solution.py:10
  140.3 7.2 %collective-permute-done = f32[16,512]{1,0:T(8,128)S(1)} collective-permute-done((f32[16,512]{1,0:T(8,128)S(1)}, f32[16,512]{1,0:T(8,128)S(1)}, u32[]{:S(2)}, u32[]{:S(2)}) %collective-permute-start) | collective-permute-done | bytes 32800 | tf_op jit(solution)/shard_map/while/body/eval_jaxpr/ppermute | solution.py:10
  149.5 7.2 %collective-permute-done = f32[16,512]{1,0:T(8,128)S(1)} collective-permute-done((f32[16,512]{1,0:T(8,128)S(1)}, f32[16,512]{1,0:T(8,128)S(1)}, u32[]{:S(2)}, u32[]{:S(2)}) %collective-permute-start) | collective-permute-done | bytes 32800 | tf_op jit(solution)/shard_map/while/body/eval_jaxpr/ppermute | solution.py:10
  158.6 7.2 %collective-permute-done = f32[16,512]{1,0:T(8,128)S(1)} collective-permute-done((f32[16,512]{1,0:T(8,128)S(1)}, f32[16,512]{1,0:T(8,128)S(1)}, u32[]{:S(2)}, u32[]{:S(2)}) %collective-permute-start) | collective-permute-done | bytes 32800 | tf_op jit(solution)/shard_map/while/body/eval_jaxpr/ppermute | solution.py:10
  167.8 7.2 %collective-permute-done = f32[16,512]{1,0:T(8,128)S(1)} collective-permute-done((f32[16,512]{1,0:T(8,128)S(1)}, f32[16,512]{1,0:T(8,128)S(1)}, u32[]{:S(2)}, u32[]{:S(2)}) %collective-permute-start) | collective-permute-done | bytes 32800 | tf_op jit(solution)/shard_map/while/body/eval_jaxpr/ppermute | solution.py:10
  176.9 7.5 %collective-permute-done = f32[16,512]{1,0:T(8,128)S(1)} collective-permute-done((f32[16,512]{1,0:T(8,128)S(1)}, f32[16,512]{1,0:T(8,128)S(1)}, u32[]{:S(2)}, u32[]{:S(2)}) %collective-permute-start) | collective-permute-done | bytes 32800 | tf_op jit(solution)/shard_map/while/body/eval_jaxpr/ppermute | solution.py:10
  186.3 7.2 %collective-permute-done = f32[16,512]{1,0:T(8,128)S(1)} collective-permute-done((f32[16,512]{1,0:T(8,128)S(1)}, f32[16,512]{1,0:T(8,128)S(1)}, u32[]{:S(2)}, u32[]{:S(2)}) %collective-permute-start) | collective-permute-done | bytes 32800 | tf_op jit(solution)/shard_map/while/body/eval_jaxpr/ppermute | solution.py:10
  195.5 7.2 %collective-permute-done = f32[16,512]{1,0:T(8,128)S(1)} collective-permute-done((f32[16,512]{1,0:T(8,128)S(1)}, f32[16,512]{1,0:T(8,128)S(1)}, u32[]{:S(2)}, u32[]{:S(2)}) %collective-permute-start) | collective-permute-done | bytes 32800 | tf_op jit(solution)/shard_map/while/body/eval_jaxpr/ppermute | solution.py:10
  204.6 7.2 %collective-permute-done = f32[16,512]{1,0:T(8,128)S(1)} collective-permute-done((f32[16,512]{1,0:T(8,128)S(1)}, f32[16,512]{1,0:T(8,128)S(1)}, u32[]{:S(2)}, u32[]{:S(2)}) %collective-permute-start) | collective-permute-done | bytes 32800 | tf_op jit(solution)/shard_map/while/body/eval_jaxpr/ppermute | solution.py:10
  213.7 7.2 %collective-permute-done = f32[16,512]{1,0:T(8,128)S(1)} collective-permute-done((f32[16,512]{1,0:T(8,128)S(1)}, f32[16,512]{1,0:T(8,128)S(1)}, u32[]{:S(2)}, u32[]{:S(2)}) %collective-permute-start) | collective-permute-done | bytes 32800 | tf_op jit(solution)/shard_map/while/body/eval_jaxpr/ppermute | solution.py:10
  222.9 7.2 %collective-permute-done = f32[16,512]{1,0:T(8,128)S(1)} collective-permute-done((f32[16,512]{1,0:T(8,128)S(1)}, f32[16,512]{1,0:T(8,128)S(1)}, u32[]{:S(2)}, u32[]{:S(2)}) %collective-permute-start) | collective-permute-done | bytes 32800 | tf_op jit(solution)/shard_map/while/body/eval_jaxpr/ppermute | solution.py:10
  232.0 7.2 %collective-permute-done = f32[16,512]{1,0:T(8,128)S(1)} collective-permute-done((f32[16,512]{1,0:T(8,128)S(1)}, f32[16,512]{1,0:T(8,128)S(1)}, u32[]{:S(2)}, u32[]{:S(2)}) %collective-permute-start) | collective-permute-done | bytes 32800 | tf_op jit(solution)/shard_map/while/body/eval_jaxpr/ppermute | solution.py:10
  241.2 7.3 %collective-permute-done = f32[16,512]{1,0:T(8,128)S(1)} collective-permute-done((f32[16,512]{1,0:T(8,128)S(1)}, f32[16,512]{1,0:T(8,128)S(1)}, u32[]{:S(2)}, u32[]{:S(2)}) %collective-permute-start) | collective-permute-done | bytes 32800 | tf_op jit(solution)/shard_map/while/body/eval_jaxpr/ppermute | solution.py:10
  250.4 7.2 %collective-permute-done = f32[16,512]{1,0:T(8,128)S(1)} collective-permute-done((f32[16,512]{1,0:T(8,128)S(1)}, f32[16,512]{1,0:T(8,128)S(1)}, u32[]{:S(2)}, u32[]{:S(2)}) %collective-permute-start) | collective-permute-done | bytes 32800 | tf_op jit(solution)/shard_map/while/body/eval_jaxpr/ppermute | solution.py:10
  259.6 7.2 %collective-permute-done = f32[16,512]{1,0:T(8,128)S(1)} collective-permute-done((f32[16,512]{1,0:T(8,128)S(1)}, f32[16,512]{1,0:T(8,128)S(1)}, u32[]{:S(2)}, u32[]{:S(2)}) %collective-permute-start) | collective-permute-done | bytes 32800 | tf_op jit(solution)/shard_map/while/body/eval_jaxpr/ppermute | solution.py:10
  268.7 7.2 %collective-permute-done = f32[16,512]{1,0:T(8,128)S(1)} collective-permute-done((f32[16,512]{1,0:T(8,128)S(1)}, f32[16,512]{1,0:T(8,128)S(1)}, u32[]{:S(2)}, u32[]{:S(2)}) %collective-permute-start) | collective-permute-done | bytes 32800 | tf_op jit(solution)/shard_map/while/body/eval_jaxpr/ppermute | solution.py:10
  277.8 7.2 %collective-permute-done = f32[16,512]{1,0:T(8,128)S(1)} collective-permute-done((f32[16,512]{1,0:T(8,128)S(1)}, f32[16,512]{1,0:T(8,128)S(1)}, u32[]{:S(2)}, u32[]{:S(2)}) %collective-permute-start) | collective-permute-done | bytes 32800 | tf_op jit(solution)/shard_map/while/body/eval_jaxpr/ppermute | solution.py:10
  287.0 7.2 %collective-permute-done = f32[16,512]{1,0:T(8,128)S(1)} collective-permute-done((f32[16,512]{1,0:T(8,128)S(1)}, f32[16,512]{1,0:T(8,128)S(1)}, u32[]{:S(2)}, u32[]{:S(2)}) %collective-permute-start) | collective-permute-done | bytes 32800 | tf_op jit(solution)/shard_map/while/body/eval_jaxpr/ppermute | solution.py:10
  296.1 7.2 %collective-permute-done = f32[16,512]{1,0:T(8,128)S(1)} collective-permute-done((f32[16,512]{1,0:T(8,128)S(1)}, f32[16,512]{1,0:T(8,128)S(1)}, u32[]{:S(2)}, u32[]{:S(2)}) %collective-permute-start) | collective-permute-done | bytes 32800 | tf_op jit(solution)/shard_map/while/body/eval_jaxpr/ppermute | solution.py:10
  305.3 7.3 %collective-permute-done = f32[16,512]{1,0:T(8,128)S(1)} collective-permute-done((f32[16,512]{1,0:T(8,128)S(1)}, f32[16,512]{1,0:T(8,128)S(1)}, u32[]{:S(2)}, u32[]{:S(2)}) %collective-permute-start) | collective-permute-done | bytes 32800 | tf_op jit(solution)/shard_map/while/body/eval_jaxpr/ppermute | solution.py:10
  314.5 7.2 %collective-permute-done = f32[16,512]{1,0:T(8,128)S(1)} collective-permute-done((f32[16,512]{1,0:T(8,128)S(1)}, f32[16,512]{1,0:T(8,128)S(1)}, u32[]{:S(2)}, u32[]{:S(2)}) %collective-permute-start) | collective-permute-done | bytes 32800 | tf_op jit(solution)/shard_map/while/body/eval_jaxpr/ppermute | solution.py:10
  323.6 7.2 %collective-permute-done = f32[16,512]{1,0:T(8,128)S(1)} collective-permute-done((f32[16,512]{1,0:T(8,128)S(1)}, f32[16,512]{1,0:T(8,128)S(1)}, u32[]{:S(2)}, u32[]{:S(2)}) %collective-permute-start) | collective-permute-done | bytes 32800 | tf_op jit(solution)/shard_map/while/body/eval_jaxpr/ppermute | solution.py:10
  332.8 7.2 %collective-permute-done = f32[16,512]{1,0:T(8,128)S(1)} collective-permute-done((f32[16,512]{1,0:T(8,128)S(1)}, f32[16,512]{1,0:T(8,128)S(1)}, u32[]{:S(2)}, u32[]{:S(2)}) %collective-permute-start) | collective-permute-done | bytes 32800 | tf_op jit(solution)/shard_map/while/body/eval_jaxpr/ppermute | solution.py:10
  341.9 7.2 %collective-permute-done = f32[16,512]{1,0:T(8,128)S(1)} collective-permute-done((f32[16,512]{1,0:T(8,128)S(1)}, f32[16,512]{1,0:T(8,128)S(1)}, u32[]{:S(2)}, u32[]{:S(2)}) %collective-permute-start) | collective-permute-done | bytes 32800 | tf_op jit(solution)/shard_map/while/body/eval_jaxpr/ppermute | solution.py:10
  351.1 7.2 %collective-permute-done = f32[16,512]{1,0:T(8,128)S(1)} collective-permute-done((f32[16,512]{1,0:T(8,128)S(1)}, f32[16,512]{1,0:T(8,128)S(1)}, u32[]{:S(2)}, u32[]{:S(2)}) %collective-permute-start) | collective-permute-done | bytes 32800 | tf_op jit(solution)/shard_map/while/body/eval_jaxpr/ppermute | solution.py:10
  360.2 7.2 %collective-permute-done = f32[16,512]{1,0:T(8,128)S(1)} collective-permute-done((f32[16,512]{1,0:T(8,128)S(1)}, f32[16,512]{1,0:T(8,128)S(1)}, u32[]{:S(2)}, u32[]{:S(2)}) %collective-permute-start) | collective-permute-done | bytes 32800 | tf_op jit(solution)/shard_map/while/body/eval_jaxpr/ppermute | solution.py:10
  369.4 7.3 %collective-permute-done = f32[16,512]{1,0:T(8,128)S(1)} collective-permute-done((f32[16,512]{1,0:T(8,128)S(1)}, f32[16,512]{1,0:T(8,128)S(1)}, u32[]{:S(2)}, u32[]{:S(2)}) %collective-permute-start) | collective-permute-done | bytes 32800 | tf_op jit(solution)/shard_map/while/body/eval_jaxpr/ppermute | solution.py:10
  378.6 7.2 %collective-permute-done = f32[16,512]{1,0:T(8,128)S(1)} collective-permute-done((f32[16,512]{1,0:T(8,128)S(1)}, f32[16,512]{1,0:T(8,128)S(1)}, u32[]{:S(2)}, u32[]{:S(2)}) %collective-permute-start) | collective-permute-done | bytes 32800 | tf_op jit(solution)/shard_map/while/body/eval_jaxpr/ppermute | solution.py:10
  387.7 7.2 %collective-permute-done = f32[16,512]{1,0:T(8,128)S(1)} collective-permute-done((f32[16,512]{1,0:T(8,128)S(1)}, f32[16,512]{1,0:T(8,128)S(1)}, u32[]{:S(2)}, u32[]{:S(2)}) %collective-permute-start) | collective-permute-done | bytes 32800 | tf_op jit(solution)/shard_map/while/body/eval_jaxpr/ppermute | solution.py:10
  396.9 7.2 %collective-permute-done = f32[16,512]{1,0:T(8,128)S(1)} collective-permute-done((f32[16,512]{1,0:T(8,128)S(1)}, f32[16,512]{1,0:T(8,128)S(1)}, u32[]{:S(2)}, u32[]{:S(2)}) %collective-permute-start) | collective-permute-done | bytes 32800 | tf_op jit(solution)/shard_map/while/body/eval_jaxpr/ppermute | solution.py:10
  406.0 7.2 %collective-permute-done = f32[16,512]{1,0:T(8,128)S(1)} collective-permute-done((f32[16,512]{1,0:T(8,128)S(1)}, f32[16,512]{1,0:T(8,128)S(1)}, u32[]{:S(2)}, u32[]{:S(2)}) %collective-permute-start) | collective-permute-done | bytes 32800 | tf_op jit(solution)/shard_map/while/body/eval_jaxpr/ppermute | solution.py:10
  415.2 7.2 %collective-permute-done = f32[16,512]{1,0:T(8,128)S(1)} collective-permute-done((f32[16,512]{1,0:T(8,128)S(1)}, f32[16,512]{1,0:T(8,128)S(1)}, u32[]{:S(2)}, u32[]{:S(2)}) %collective-permute-start) | collective-permute-done | bytes 32800 | tf_op jit(solution)/shard_map/while/body/eval_jaxpr/ppermute | solution.py:10
  424.3 7.2 %collective-permute-done = f32[16,512]{1,0:T(8,128)S(1)} collective-permute-done((f32[16,512]{1,0:T(8,128)S(1)}, f32[16,512]{1,0:T(8,128)S(1)}, u32[]{:S(2)}, u32[]{:S(2)}) %collective-permute-start) | collective-permute-done | bytes 32800 | tf_op jit(solution)/shard_map/while/body/eval_jaxpr/ppermute | solution.py:10
  433.4 7.3 %collective-permute-done = f32[16,512]{1,0:T(8,128)S(1)} collective-permute-done((f32[16,512]{1,0:T(8,128)S(1)}, f32[16,512]{1,0:T(8,128)S(1)}, u32[]{:S(2)}, u32[]{:S(2)}) %collective-permute-start) | collective-permute-done | bytes 32800 | tf_op jit(solution)/shard_map/while/body/eval_jaxpr/ppermute | solution.py:10
  442.7 7.2 %collective-permute-done = f32[16,512]{1,0:T(8,128)S(1)} collective-permute-done((f32[16,512]{1,0:T(8,128)S(1)}, f32[16,512]{1,0:T(8,128)S(1)}, u32[]{:S(2)}, u32[]{:S(2)}) %collective-permute-start) | collective-permute-done | bytes 32800 | tf_op jit(solution)/shard_map/while/body/eval_jaxpr/ppermute | solution.py:10
  451.8 7.2 %collective-permute-done = f32[16,512]{1,0:T(8,128)S(1)} collective-permute-done((f32[16,512]{1,0:T(8,128)S(1)}, f32[16,512]{1,0:T(8,128)S(1)}, u32[]{:S(2)}, u32[]{:S(2)}) %collective-permute-start) | collective-permute-done | bytes 32800 | tf_op jit(solution)/shard_map/while/body/eval_jaxpr/ppermute | solution.py:10
  461.0 7.2 %collective-permute-done = f32[16,512]{1,0:T(8,128)S(1)} collective-permute-done((f32[16,512]{1,0:T(8,128)S(1)}, f32[16,512]{1,0:T(8,128)S(1)}, u32[]{:S(2)}, u32[]{:S(2)}) %collective-permute-start) | collective-permute-done | bytes 32800 | tf_op jit(solution)/shard_map/while/body/eval_jaxpr/ppermute | solution.py:10
  470.1 7.2 %collective-permute-done = f32[16,512]{1,0:T(8,128)S(1)} collective-permute-done((f32[16,512]{1,0:T(8,128)S(1)}, f32[16,512]{1,0:T(8,128)S(1)}, u32[]{:S(2)}, u32[]{:S(2)}) %collective-permute-start) | collective-permute-done | bytes 32800 | tf_op jit(solution)/shard_map/while/body/eval_jaxpr/ppermute | solution.py:10
  479.3 7.2 %collective-permute-done = f32[16,512]{1,0:T(8,128)S(1)} collective-permute-done((f32[16,512]{1,0:T(8,128)S(1)}, f32[16,512]{1,0:T(8,128)S(1)}, u32[]{:S(2)}, u32[]{:S(2)}) %collective-permute-start) | collective-permute-done | bytes 32800 | tf_op jit(solution)/shard_map/while/body/eval_jaxpr/ppermute | solution.py:10
  488.4 7.2 %collective-permute-done = f32[16,512]{1,0:T(8,128)S(1)} collective-permute-done((f32[16,512]{1,0:T(8,128)S(1)}, f32[16,512]{1,0:T(8,128)S(1)}, u32[]{:S(2)}, u32[]{:S(2)}) %collective-permute-start) | collective-permute-done | bytes 32800 | tf_op jit(solution)/shard_map/while/body/eval_jaxpr/ppermute | solution.py:10
  497.5 7.3 %collective-permute-done = f32[16,512]{1,0:T(8,128)S(1)} collective-permute-done((f32[16,512]{1,0:T(8,128)S(1)}, f32[16,512]{1,0:T(8,128)S(1)}, u32[]{:S(2)}, u32[]{:S(2)}) %collective-permute-start) | collective-permute-done | bytes 32800 | tf_op jit(solution)/shard_map/while/body/eval_jaxpr/ppermute | solution.py:10
  506.8 7.2 %collective-permute-done = f32[16,512]{1,0:T(8,128)S(1)} collective-permute-done((f32[16,512]{1,0:T(8,128)S(1)}, f32[16,512]{1,0:T(8,128)S(1)}, u32[]{:S(2)}, u32[]{:S(2)}) %collective-permute-start) | collective-permute-done | bytes 32800 | tf_op jit(solution)/shard_map/while/body/eval_jaxpr/ppermute | solution.py:10
  515.9 7.2 %collective-permute-done = f32[16,512]{1,0:T(8,128)S(1)} collective-permute-done((f32[16,512]{1,0:T(8,128)S(1)}, f32[16,512]{1,0:T(8,128)S(1)}, u32[]{:S(2)}, u32[]{:S(2)}) %collective-permute-start) | collective-permute-done | bytes 32800 | tf_op jit(solution)/shard_map/while/body/eval_jaxpr/ppermute | solution.py:10
  525.1 7.2 %collective-permute-done = f32[16,512]{1,0:T(8,128)S(1)} collective-permute-done((f32[16,512]{1,0:T(8,128)S(1)}, f32[16,512]{1,0:T(8,128)S(1)}, u32[]{:S(2)}, u32[]{:S(2)}) %collective-permute-start) | collective-permute-done | bytes 32800 | tf_op jit(solution)/shard_map/while/body/eval_jaxpr/ppermute | solution.py:10
  534.2 7.2 %collective-permute-done = f32[16,512]{1,0:T(8,128)S(1)} collective-permute-done((f32[16,512]{1,0:T(8,128)S(1)}, f32[16,512]{1,0:T(8,128)S(1)}, u32[]{:S(2)}, u32[]{:S(2)}) %collective-permute-start) | collective-permute-done | bytes 32800 | tf_op jit(solution)/shard_map/while/body/eval_jaxpr/ppermute | solution.py:10
  543.4 7.2 %collective-permute-done = f32[16,512]{1,0:T(8,128)S(1)} collective-permute-done((f32[16,512]{1,0:T(8,128)S(1)}, f32[16,512]{1,0:T(8,128)S(1)}, u32[]{:S(2)}, u32[]{:S(2)}) %collective-permute-start) | collective-permute-done | bytes 32800 | tf_op jit(solution)/shard_map/while/body/eval_jaxpr/ppermute | solution.py:10
  552.5 7.2 %collective-permute-done = f32[16,512]{1,0:T(8,128)S(1)} collective-permute-done((f32[16,512]{1,0:T(8,128)S(1)}, f32[16,512]{1,0:T(8,128)S(1)}, u32[]{:S(2)}, u32[]{:S(2)}) %collective-permute-start) | collective-permute-done | bytes 32800 | tf_op jit(solution)/shard_map/while/body/eval_jaxpr/ppermute | solution.py:10
  561.6 7.3 %collective-permute-done = f32[16,512]{1,0:T(8,128)S(1)} collective-permute-done((f32[16,512]{1,0:T(8,128)S(1)}, f32[16,512]{1,0:T(8,128)S(1)}, u32[]{:S(2)}, u32[]{:S(2)}) %collective-permute-start) | collective-permute-done | bytes 32800 | tf_op jit(solution)/shard_map/while/body/eval_jaxpr/ppermute | solution.py:10
  570.9 7.2 %collective-permute-done = f32[16,512]{1,0:T(8,128)S(1)} collective-permute-done((f32[16,512]{1,0:T(8,128)S(1)}, f32[16,512]{1,0:T(8,128)S(1)}, u32[]{:S(2)}, u32[]{:S(2)}) %collective-permute-start) | collective-permute-done | bytes 32800 | tf_op jit(solution)/shard_map/while/body/eval_jaxpr/ppermute | solution.py:10
  589.2 7.2 %collective-permute-done = f32[16,512]{1,0:T(8,128)S(1)} collective-permute-done((f32[16,512]{1,0:T(8,128)S(1)}, f32[16,512]{1,0:T(8,128)S(1)}, u32[]{:S(2)}, u32[]{:S(2)}) %collective-permute-start) | collective-permute-done | bytes 32800 | tf_op jit(solution)/shard_map/while/body/eval_jaxpr/ppermute | solution.py:10
  598.3 7.2 %collective-permute-done = f32[16,512]{1,0:T(8,128)S(1)} collective-permute-done((f32[16,512]{1,0:T(8,128)S(1)}, f32[16,512]{1,0:T(8,128)S(1)}, u32[]{:S(2)}, u32[]{:S(2)}) %collective-permute-start) | collective-permute-done | bytes 32800 | tf_op jit(solution)/shard_map/while/body/eval_jaxpr/ppermute | solution.py:10
  607.5 7.2 %collective-permute-done = f32[16,512]{1,0:T(8,128)S(1)} collective-permute-done((f32[16,512]{1,0:T(8,128)S(1)}, f32[16,512]{1,0:T(8,128)S(1)}, u32[]{:S(2)}, u32[]{:S(2)}) %collective-permute-start) | collective-permute-done | bytes 32800 | tf_op jit(solution)/shard_map/while/body/eval_jaxpr/ppermute | solution.py:10
  616.6 7.2 %collective-permute-done = f32[16,512]{1,0:T(8,128)S(1)} collective-permute-done((f32[16,512]{1,0:T(8,128)S(1)}, f32[16,512]{1,0:T(8,128)S(1)}, u32[]{:S(2)}, u32[]{:S(2)}) %collective-permute-start) | collective-permute-done | bytes 32800 | tf_op jit(solution)/shard_map/while/body/eval_jaxpr/ppermute | solution.py:10
  634.9 7.2 %collective-permute-done = f32[16,512]{1,0:T(8,128)S(1)} collective-permute-done((f32[16,512]{1,0:T(8,128)S(1)}, f32[16,512]{1,0:T(8,128)S(1)}, u32[]{:S(2)}, u32[]{:S(2)}) %collective-permute-start) | collective-permute-done | bytes 32800 | tf_op jit(solution)/shard_map/while/body/eval_jaxpr/ppermute | solution.py:10
  644.0 7.2 %collective-permute-done = f32[16,512]{1,0:T(8,128)S(1)} collective-permute-done((f32[16,512]{1,0:T(8,128)S(1)}, f32[16,512]{1,0:T(8,128)S(1)}, u32[]{:S(2)}, u32[]{:S(2)}) %collective-permute-start) | collective-permute-done | bytes 32800 | tf_op jit(solution)/shard_map/while/body/eval_jaxpr/ppermute | solution.py:10
  669.2 11.2 %fusion.10 = f32[4,128,512]{2,0,1:T(4,128)S(1)} fusion(f32[128,1,512]{2,1,0:T(1,128)S(1)} %copy-done.6, f32[512,4,128]{0,1,2:T(4,128)} %copy.226, f32[512,4,128]{0,1,2:T(4,128)S(1)} %copy.223, bf16[4,128,512]{2,1,0:T(8,128)(2,1)S(1)} %bitcast.76), kind=kOutput, calls=%fused_computation.20 | convolution fusion | flops 203423744 | bytes 3932160 | tf_op jit(solution)/shard_map/conv_general_dilated | solution.py:14
  (240 shorter events, 213.2 us)
Async XLA Ops:
  17.3 11.4 %collective-permute-start.1 = (bf16[6,512]{1,0:T(8,128)(2,1)S(1)}, bf16[6,512]{1,0:T(8,128)(2,1)S(1)}, u32[]{:S(2)}, u32[]{:S(2)}) collective-permute-start(bf16[6,512]{1,0:T(8,128)(2,1)S(1)} %slice.108), channel_id=1, source_target_pairs={{0,8},{8,16},{16,24},{24,32},{32,40},{40,48},{48,56},{56,64},{64,7... | collective-permute-start | bytes 18440 | tf_op jit(solution)/shard_map/ppermute | solution.py:10
  31.9 10.2 %collective-permute-start.2 = (bf16[127,512]{1,0:T(8,128)(2,1)S(1)}, bf16[127,512]{1,0:T(8,128)(2,1)S(1)}, u32[]{:S(2)}, u32[]{:S(2)}) collective-permute-start(bf16[127,512]{1,0:T(8,128)(2,1)S(1)} %slice_bitcast_fusion.3), channel_id=1, source_target_pairs={{0,8},{8,16},{16,24},{24,32},{32,40},{40,48},{48,56},{56,64},{64,7... | collective-permute-start | bytes 390152 | tf_op jit(solution)/shard_map/ppermute | solution.py:10
  53.9 12.3 %collective-permute-start.3 = (bf16[6,512]{1,0:T(8,128)(2,1)S(1)}, bf16[6,512]{1,0:T(8,128)(2,1)S(1)}, u32[]{:S(2)}, u32[]{:S(2)}) collective-permute-start(bf16[6,512]{1,0:T(8,128)(2,1)S(1)} %bitcast.87), channel_id=1, source_target_pairs={{0,8},{8,16},{16,24},{24,32},{32,40},{40,48},{48,56},{56,64},{64,7... | collective-permute-start | bytes 18440 | tf_op jit(solution)/shard_map/ppermute | solution.py:10
  83.4 9.1 %collective-permute-start = (f32[16,512]{1,0:T(8,128)S(1)}, f32[16,512]{1,0:T(8,128)S(1)}, u32[]{:S(2)}, u32[]{:S(2)}) collective-permute-start(f32[16,512]{1,0:T(8,128)S(1)} %multiply_add_fusion.2), channel_id=1, source_target_pairs={{0,8},{8,16},{16,24},{24,32},{32,40},{40,48},{48,56},{56,64},{64,7... | collective-permute-start | bytes 98312 | tf_op jit(solution)/shard_map/while/body/eval_jaxpr/ppermute | solution.py:10
  92.5 9.1 %collective-permute-start = (f32[16,512]{1,0:T(8,128)S(1)}, f32[16,512]{1,0:T(8,128)S(1)}, u32[]{:S(2)}, u32[]{:S(2)}) collective-permute-start(f32[16,512]{1,0:T(8,128)S(1)} %multiply_add_fusion.2), channel_id=1, source_target_pairs={{0,8},{8,16},{16,24},{24,32},{32,40},{40,48},{48,56},{56,64},{64,7... | collective-permute-start | bytes 98312 | tf_op jit(solution)/shard_map/while/body/eval_jaxpr/ppermute | solution.py:10
  101.7 9.1 %collective-permute-start = (f32[16,512]{1,0:T(8,128)S(1)}, f32[16,512]{1,0:T(8,128)S(1)}, u32[]{:S(2)}, u32[]{:S(2)}) collective-permute-start(f32[16,512]{1,0:T(8,128)S(1)} %multiply_add_fusion.2), channel_id=1, source_target_pairs={{0,8},{8,16},{16,24},{24,32},{32,40},{40,48},{48,56},{56,64},{64,7... | collective-permute-start | bytes 98312 | tf_op jit(solution)/shard_map/while/body/eval_jaxpr/ppermute | solution.py:10
  110.8 9.3 %collective-permute-start = (f32[16,512]{1,0:T(8,128)S(1)}, f32[16,512]{1,0:T(8,128)S(1)}, u32[]{:S(2)}, u32[]{:S(2)}) collective-permute-start(f32[16,512]{1,0:T(8,128)S(1)} %multiply_add_fusion.2), channel_id=1, source_target_pairs={{0,8},{8,16},{16,24},{24,32},{32,40},{40,48},{48,56},{56,64},{64,7... | collective-permute-start | bytes 98312 | tf_op jit(solution)/shard_map/while/body/eval_jaxpr/ppermute | solution.py:10
  120.1 9.1 %collective-permute-start = (f32[16,512]{1,0:T(8,128)S(1)}, f32[16,512]{1,0:T(8,128)S(1)}, u32[]{:S(2)}, u32[]{:S(2)}) collective-permute-start(f32[16,512]{1,0:T(8,128)S(1)} %multiply_add_fusion.2), channel_id=1, source_target_pairs={{0,8},{8,16},{16,24},{24,32},{32,40},{40,48},{48,56},{56,64},{64,7... | collective-permute-start | bytes 98312 | tf_op jit(solution)/shard_map/while/body/eval_jaxpr/ppermute | solution.py:10
  129.3 9.1 %collective-permute-start = (f32[16,512]{1,0:T(8,128)S(1)}, f32[16,512]{1,0:T(8,128)S(1)}, u32[]{:S(2)}, u32[]{:S(2)}) collective-permute-start(f32[16,512]{1,0:T(8,128)S(1)} %multiply_add_fusion.2), channel_id=1, source_target_pairs={{0,8},{8,16},{16,24},{24,32},{32,40},{40,48},{48,56},{56,64},{64,7... | collective-permute-start | bytes 98312 | tf_op jit(solution)/shard_map/while/body/eval_jaxpr/ppermute | solution.py:10
  138.4 9.1 %collective-permute-start = (f32[16,512]{1,0:T(8,128)S(1)}, f32[16,512]{1,0:T(8,128)S(1)}, u32[]{:S(2)}, u32[]{:S(2)}) collective-permute-start(f32[16,512]{1,0:T(8,128)S(1)} %multiply_add_fusion.2), channel_id=1, source_target_pairs={{0,8},{8,16},{16,24},{24,32},{32,40},{40,48},{48,56},{56,64},{64,7... | collective-permute-start | bytes 98312 | tf_op jit(solution)/shard_map/while/body/eval_jaxpr/ppermute | solution.py:10
  147.5 9.1 %collective-permute-start = (f32[16,512]{1,0:T(8,128)S(1)}, f32[16,512]{1,0:T(8,128)S(1)}, u32[]{:S(2)}, u32[]{:S(2)}) collective-permute-start(f32[16,512]{1,0:T(8,128)S(1)} %multiply_add_fusion.2), channel_id=1, source_target_pairs={{0,8},{8,16},{16,24},{24,32},{32,40},{40,48},{48,56},{56,64},{64,7... | collective-permute-start | bytes 98312 | tf_op jit(solution)/shard_map/while/body/eval_jaxpr/ppermute | solution.py:10
  156.7 9.1 %collective-permute-start = (f32[16,512]{1,0:T(8,128)S(1)}, f32[16,512]{1,0:T(8,128)S(1)}, u32[]{:S(2)}, u32[]{:S(2)}) collective-permute-start(f32[16,512]{1,0:T(8,128)S(1)} %multiply_add_fusion.2), channel_id=1, source_target_pairs={{0,8},{8,16},{16,24},{24,32},{32,40},{40,48},{48,56},{56,64},{64,7... | collective-permute-start | bytes 98312 | tf_op jit(solution)/shard_map/while/body/eval_jaxpr/ppermute | solution.py:10
  165.8 9.1 %collective-permute-start = (f32[16,512]{1,0:T(8,128)S(1)}, f32[16,512]{1,0:T(8,128)S(1)}, u32[]{:S(2)}, u32[]{:S(2)}) collective-permute-start(f32[16,512]{1,0:T(8,128)S(1)} %multiply_add_fusion.2), channel_id=1, source_target_pairs={{0,8},{8,16},{16,24},{24,32},{32,40},{40,48},{48,56},{56,64},{64,7... | collective-permute-start | bytes 98312 | tf_op jit(solution)/shard_map/while/body/eval_jaxpr/ppermute | solution.py:10
  175.0 9.4 %collective-permute-start = (f32[16,512]{1,0:T(8,128)S(1)}, f32[16,512]{1,0:T(8,128)S(1)}, u32[]{:S(2)}, u32[]{:S(2)}) collective-permute-start(f32[16,512]{1,0:T(8,128)S(1)} %multiply_add_fusion.2), channel_id=1, source_target_pairs={{0,8},{8,16},{16,24},{24,32},{32,40},{40,48},{48,56},{56,64},{64,7... | collective-permute-start | bytes 98312 | tf_op jit(solution)/shard_map/while/body/eval_jaxpr/ppermute | solution.py:10
  184.4 9.1 %collective-permute-start = (f32[16,512]{1,0:T(8,128)S(1)}, f32[16,512]{1,0:T(8,128)S(1)}, u32[]{:S(2)}, u32[]{:S(2)}) collective-permute-start(f32[16,512]{1,0:T(8,128)S(1)} %multiply_add_fusion.2), channel_id=1, source_target_pairs={{0,8},{8,16},{16,24},{24,32},{32,40},{40,48},{48,56},{56,64},{64,7... | collective-permute-start | bytes 98312 | tf_op jit(solution)/shard_map/while/body/eval_jaxpr/ppermute | solution.py:10
  193.5 9.1 %collective-permute-start = (f32[16,512]{1,0:T(8,128)S(1)}, f32[16,512]{1,0:T(8,128)S(1)}, u32[]{:S(2)}, u32[]{:S(2)}) collective-permute-start(f32[16,512]{1,0:T(8,128)S(1)} %multiply_add_fusion.2), channel_id=1, source_target_pairs={{0,8},{8,16},{16,24},{24,32},{32,40},{40,48},{48,56},{56,64},{64,7... | collective-permute-start | bytes 98312 | tf_op jit(solution)/shard_map/while/body/eval_jaxpr/ppermute | solution.py:10
  202.7 9.1 %collective-permute-start = (f32[16,512]{1,0:T(8,128)S(1)}, f32[16,512]{1,0:T(8,128)S(1)}, u32[]{:S(2)}, u32[]{:S(2)}) collective-permute-start(f32[16,512]{1,0:T(8,128)S(1)} %multiply_add_fusion.2), channel_id=1, source_target_pairs={{0,8},{8,16},{16,24},{24,32},{32,40},{40,48},{48,56},{56,64},{64,7... | collective-permute-start | bytes 98312 | tf_op jit(solution)/shard_map/while/body/eval_jaxpr/ppermute | solution.py:10
  211.8 9.1 %collective-permute-start = (f32[16,512]{1,0:T(8,128)S(1)}, f32[16,512]{1,0:T(8,128)S(1)}, u32[]{:S(2)}, u32[]{:S(2)}) collective-permute-start(f32[16,512]{1,0:T(8,128)S(1)} %multiply_add_fusion.2), channel_id=1, source_target_pairs={{0,8},{8,16},{16,24},{24,32},{32,40},{40,48},{48,56},{56,64},{64,7... | collective-permute-start | bytes 98312 | tf_op jit(solution)/shard_map/while/body/eval_jaxpr/ppermute | solution.py:10
  220.9 9.1 %collective-permute-start = (f32[16,512]{1,0:T(8,128)S(1)}, f32[16,512]{1,0:T(8,128)S(1)}, u32[]{:S(2)}, u32[]{:S(2)}) collective-permute-start(f32[16,512]{1,0:T(8,128)S(1)} %multiply_add_fusion.2), channel_id=1, source_target_pairs={{0,8},{8,16},{16,24},{24,32},{32,40},{40,48},{48,56},{56,64},{64,7... | collective-permute-start | bytes 98312 | tf_op jit(solution)/shard_map/while/body/eval_jaxpr/ppermute | solution.py:10
  230.1 9.1 %collective-permute-start = (f32[16,512]{1,0:T(8,128)S(1)}, f32[16,512]{1,0:T(8,128)S(1)}, u32[]{:S(2)}, u32[]{:S(2)}) collective-permute-start(f32[16,512]{1,0:T(8,128)S(1)} %multiply_add_fusion.2), channel_id=1, source_target_pairs={{0,8},{8,16},{16,24},{24,32},{32,40},{40,48},{48,56},{56,64},{64,7... | collective-permute-start | bytes 98312 | tf_op jit(solution)/shard_map/while/body/eval_jaxpr/ppermute | solution.py:10
  239.2 9.2 %collective-permute-start = (f32[16,512]{1,0:T(8,128)S(1)}, f32[16,512]{1,0:T(8,128)S(1)}, u32[]{:S(2)}, u32[]{:S(2)}) collective-permute-start(f32[16,512]{1,0:T(8,128)S(1)} %multiply_add_fusion.2), channel_id=1, source_target_pairs={{0,8},{8,16},{16,24},{24,32},{32,40},{40,48},{48,56},{56,64},{64,7... | collective-permute-start | bytes 98312 | tf_op jit(solution)/shard_map/while/body/eval_jaxpr/ppermute | solution.py:10
  248.5 9.1 %collective-permute-start = (f32[16,512]{1,0:T(8,128)S(1)}, f32[16,512]{1,0:T(8,128)S(1)}, u32[]{:S(2)}, u32[]{:S(2)}) collective-permute-start(f32[16,512]{1,0:T(8,128)S(1)} %multiply_add_fusion.2), channel_id=1, source_target_pairs={{0,8},{8,16},{16,24},{24,32},{32,40},{40,48},{48,56},{56,64},{64,7... | collective-permute-start | bytes 98312 | tf_op jit(solution)/shard_map/while/body/eval_jaxpr/ppermute | solution.py:10
  257.6 9.1 %collective-permute-start = (f32[16,512]{1,0:T(8,128)S(1)}, f32[16,512]{1,0:T(8,128)S(1)}, u32[]{:S(2)}, u32[]{:S(2)}) collective-permute-start(f32[16,512]{1,0:T(8,128)S(1)} %multiply_add_fusion.2), channel_id=1, source_target_pairs={{0,8},{8,16},{16,24},{24,32},{32,40},{40,48},{48,56},{56,64},{64,7... | collective-permute-start | bytes 98312 | tf_op jit(solution)/shard_map/while/body/eval_jaxpr/ppermute | solution.py:10
  266.8 9.1 %collective-permute-start = (f32[16,512]{1,0:T(8,128)S(1)}, f32[16,512]{1,0:T(8,128)S(1)}, u32[]{:S(2)}, u32[]{:S(2)}) collective-permute-start(f32[16,512]{1,0:T(8,128)S(1)} %multiply_add_fusion.2), channel_id=1, source_target_pairs={{0,8},{8,16},{16,24},{24,32},{32,40},{40,48},{48,56},{56,64},{64,7... | collective-permute-start | bytes 98312 | tf_op jit(solution)/shard_map/while/body/eval_jaxpr/ppermute | solution.py:10
  275.9 9.1 %collective-permute-start = (f32[16,512]{1,0:T(8,128)S(1)}, f32[16,512]{1,0:T(8,128)S(1)}, u32[]{:S(2)}, u32[]{:S(2)}) collective-permute-start(f32[16,512]{1,0:T(8,128)S(1)} %multiply_add_fusion.2), channel_id=1, source_target_pairs={{0,8},{8,16},{16,24},{24,32},{32,40},{40,48},{48,56},{56,64},{64,7... | collective-permute-start | bytes 98312 | tf_op jit(solution)/shard_map/while/body/eval_jaxpr/ppermute | solution.py:10
  285.0 9.1 %collective-permute-start = (f32[16,512]{1,0:T(8,128)S(1)}, f32[16,512]{1,0:T(8,128)S(1)}, u32[]{:S(2)}, u32[]{:S(2)}) collective-permute-start(f32[16,512]{1,0:T(8,128)S(1)} %multiply_add_fusion.2), channel_id=1, source_target_pairs={{0,8},{8,16},{16,24},{24,32},{32,40},{40,48},{48,56},{56,64},{64,7... | collective-permute-start | bytes 98312 | tf_op jit(solution)/shard_map/while/body/eval_jaxpr/ppermute | solution.py:10
  294.2 9.1 %collective-permute-start = (f32[16,512]{1,0:T(8,128)S(1)}, f32[16,512]{1,0:T(8,128)S(1)}, u32[]{:S(2)}, u32[]{:S(2)}) collective-permute-start(f32[16,512]{1,0:T(8,128)S(1)} %multiply_add_fusion.2), channel_id=1, source_target_pairs={{0,8},{8,16},{16,24},{24,32},{32,40},{40,48},{48,56},{56,64},{64,7... | collective-permute-start | bytes 98312 | tf_op jit(solution)/shard_map/while/body/eval_jaxpr/ppermute | solution.py:10
  303.3 9.2 %collective-permute-start = (f32[16,512]{1,0:T(8,128)S(1)}, f32[16,512]{1,0:T(8,128)S(1)}, u32[]{:S(2)}, u32[]{:S(2)}) collective-permute-start(f32[16,512]{1,0:T(8,128)S(1)} %multiply_add_fusion.2), channel_id=1, source_target_pairs={{0,8},{8,16},{16,24},{24,32},{32,40},{40,48},{48,56},{56,64},{64,7... | collective-permute-start | bytes 98312 | tf_op jit(solution)/shard_map/while/body/eval_jaxpr/ppermute | solution.py:10
  312.6 9.1 %collective-permute-start = (f32[16,512]{1,0:T(8,128)S(1)}, f32[16,512]{1,0:T(8,128)S(1)}, u32[]{:S(2)}, u32[]{:S(2)}) collective-permute-start(f32[16,512]{1,0:T(8,128)S(1)} %multiply_add_fusion.2), channel_id=1, source_target_pairs={{0,8},{8,16},{16,24},{24,32},{32,40},{40,48},{48,56},{56,64},{64,7... | collective-permute-start | bytes 98312 | tf_op jit(solution)/shard_map/while/body/eval_jaxpr/ppermute | solution.py:10
  321.7 9.1 %collective-permute-start = (f32[16,512]{1,0:T(8,128)S(1)}, f32[16,512]{1,0:T(8,128)S(1)}, u32[]{:S(2)}, u32[]{:S(2)}) collective-permute-start(f32[16,512]{1,0:T(8,128)S(1)} %multiply_add_fusion.2), channel_id=1, source_target_pairs={{0,8},{8,16},{16,24},{24,32},{32,40},{40,48},{48,56},{56,64},{64,7... | collective-permute-start | bytes 98312 | tf_op jit(solution)/shard_map/while/body/eval_jaxpr/ppermute | solution.py:10
  330.9 9.1 %collective-permute-start = (f32[16,512]{1,0:T(8,128)S(1)}, f32[16,512]{1,0:T(8,128)S(1)}, u32[]{:S(2)}, u32[]{:S(2)}) collective-permute-start(f32[16,512]{1,0:T(8,128)S(1)} %multiply_add_fusion.2), channel_id=1, source_target_pairs={{0,8},{8,16},{16,24},{24,32},{32,40},{40,48},{48,56},{56,64},{64,7... | collective-permute-start | bytes 98312 | tf_op jit(solution)/shard_map/while/body/eval_jaxpr/ppermute | solution.py:10
  340.0 9.1 %collective-permute-start = (f32[16,512]{1,0:T(8,128)S(1)}, f32[16,512]{1,0:T(8,128)S(1)}, u32[]{:S(2)}, u32[]{:S(2)}) collective-permute-start(f32[16,512]{1,0:T(8,128)S(1)} %multiply_add_fusion.2), channel_id=1, source_target_pairs={{0,8},{8,16},{16,24},{24,32},{32,40},{40,48},{48,56},{56,64},{64,7... | collective-permute-start | bytes 98312 | tf_op jit(solution)/shard_map/while/body/eval_jaxpr/ppermute | solution.py:10
  349.1 9.1 %collective-permute-start = (f32[16,512]{1,0:T(8,128)S(1)}, f32[16,512]{1,0:T(8,128)S(1)}, u32[]{:S(2)}, u32[]{:S(2)}) collective-permute-start(f32[16,512]{1,0:T(8,128)S(1)} %multiply_add_fusion.2), channel_id=1, source_target_pairs={{0,8},{8,16},{16,24},{24,32},{32,40},{40,48},{48,56},{56,64},{64,7... | collective-permute-start | bytes 98312 | tf_op jit(solution)/shard_map/while/body/eval_jaxpr/ppermute | solution.py:10
  358.3 9.1 %collective-permute-start = (f32[16,512]{1,0:T(8,128)S(1)}, f32[16,512]{1,0:T(8,128)S(1)}, u32[]{:S(2)}, u32[]{:S(2)}) collective-permute-start(f32[16,512]{1,0:T(8,128)S(1)} %multiply_add_fusion.2), channel_id=1, source_target_pairs={{0,8},{8,16},{16,24},{24,32},{32,40},{40,48},{48,56},{56,64},{64,7... | collective-permute-start | bytes 98312 | tf_op jit(solution)/shard_map/while/body/eval_jaxpr/ppermute | solution.py:10
  367.4 9.2 %collective-permute-start = (f32[16,512]{1,0:T(8,128)S(1)}, f32[16,512]{1,0:T(8,128)S(1)}, u32[]{:S(2)}, u32[]{:S(2)}) collective-permute-start(f32[16,512]{1,0:T(8,128)S(1)} %multiply_add_fusion.2), channel_id=1, source_target_pairs={{0,8},{8,16},{16,24},{24,32},{32,40},{40,48},{48,56},{56,64},{64,7... | collective-permute-start | bytes 98312 | tf_op jit(solution)/shard_map/while/body/eval_jaxpr/ppermute | solution.py:10
  376.7 9.1 %collective-permute-start = (f32[16,512]{1,0:T(8,128)S(1)}, f32[16,512]{1,0:T(8,128)S(1)}, u32[]{:S(2)}, u32[]{:S(2)}) collective-permute-start(f32[16,512]{1,0:T(8,128)S(1)} %multiply_add_fusion.2), channel_id=1, source_target_pairs={{0,8},{8,16},{16,24},{24,32},{32,40},{40,48},{48,56},{56,64},{64,7... | collective-permute-start | bytes 98312 | tf_op jit(solution)/shard_map/while/body/eval_jaxpr/ppermute | solution.py:10
  385.8 9.1 %collective-permute-start = (f32[16,512]{1,0:T(8,128)S(1)}, f32[16,512]{1,0:T(8,128)S(1)}, u32[]{:S(2)}, u32[]{:S(2)}) collective-permute-start(f32[16,512]{1,0:T(8,128)S(1)} %multiply_add_fusion.2), channel_id=1, source_target_pairs={{0,8},{8,16},{16,24},{24,32},{32,40},{40,48},{48,56},{56,64},{64,7... | collective-permute-start | bytes 98312 | tf_op jit(solution)/shard_map/while/body/eval_jaxpr/ppermute | solution.py:10
  395.0 9.1 %collective-permute-start = (f32[16,512]{1,0:T(8,128)S(1)}, f32[16,512]{1,0:T(8,128)S(1)}, u32[]{:S(2)}, u32[]{:S(2)}) collective-permute-start(f32[16,512]{1,0:T(8,128)S(1)} %multiply_add_fusion.2), channel_id=1, source_target_pairs={{0,8},{8,16},{16,24},{24,32},{32,40},{40,48},{48,56},{56,64},{64,7... | collective-permute-start | bytes 98312 | tf_op jit(solution)/shard_map/while/body/eval_jaxpr/ppermute | solution.py:10
  404.1 9.1 %collective-permute-start = (f32[16,512]{1,0:T(8,128)S(1)}, f32[16,512]{1,0:T(8,128)S(1)}, u32[]{:S(2)}, u32[]{:S(2)}) collective-permute-start(f32[16,512]{1,0:T(8,128)S(1)} %multiply_add_fusion.2), channel_id=1, source_target_pairs={{0,8},{8,16},{16,24},{24,32},{32,40},{40,48},{48,56},{56,64},{64,7... | collective-permute-start | bytes 98312 | tf_op jit(solution)/shard_map/while/body/eval_jaxpr/ppermute | solution.py:10
  413.2 9.1 %collective-permute-start = (f32[16,512]{1,0:T(8,128)S(1)}, f32[16,512]{1,0:T(8,128)S(1)}, u32[]{:S(2)}, u32[]{:S(2)}) collective-permute-start(f32[16,512]{1,0:T(8,128)S(1)} %multiply_add_fusion.2), channel_id=1, source_target_pairs={{0,8},{8,16},{16,24},{24,32},{32,40},{40,48},{48,56},{56,64},{64,7... | collective-permute-start | bytes 98312 | tf_op jit(solution)/shard_map/while/body/eval_jaxpr/ppermute | solution.py:10
  422.4 9.1 %collective-permute-start = (f32[16,512]{1,0:T(8,128)S(1)}, f32[16,512]{1,0:T(8,128)S(1)}, u32[]{:S(2)}, u32[]{:S(2)}) collective-permute-start(f32[16,512]{1,0:T(8,128)S(1)} %multiply_add_fusion.2), channel_id=1, source_target_pairs={{0,8},{8,16},{16,24},{24,32},{32,40},{40,48},{48,56},{56,64},{64,7... | collective-permute-start | bytes 98312 | tf_op jit(solution)/shard_map/while/body/eval_jaxpr/ppermute | solution.py:10
  431.5 9.2 %collective-permute-start = (f32[16,512]{1,0:T(8,128)S(1)}, f32[16,512]{1,0:T(8,128)S(1)}, u32[]{:S(2)}, u32[]{:S(2)}) collective-permute-start(f32[16,512]{1,0:T(8,128)S(1)} %multiply_add_fusion.2), channel_id=1, source_target_pairs={{0,8},{8,16},{16,24},{24,32},{32,40},{40,48},{48,56},{56,64},{64,7... | collective-permute-start | bytes 98312 | tf_op jit(solution)/shard_map/while/body/eval_jaxpr/ppermute | solution.py:10
  440.8 9.1 %collective-permute-start = (f32[16,512]{1,0:T(8,128)S(1)}, f32[16,512]{1,0:T(8,128)S(1)}, u32[]{:S(2)}, u32[]{:S(2)}) collective-permute-start(f32[16,512]{1,0:T(8,128)S(1)} %multiply_add_fusion.2), channel_id=1, source_target_pairs={{0,8},{8,16},{16,24},{24,32},{32,40},{40,48},{48,56},{56,64},{64,7... | collective-permute-start | bytes 98312 | tf_op jit(solution)/shard_map/while/body/eval_jaxpr/ppermute | solution.py:10
  449.9 9.1 %collective-permute-start = (f32[16,512]{1,0:T(8,128)S(1)}, f32[16,512]{1,0:T(8,128)S(1)}, u32[]{:S(2)}, u32[]{:S(2)}) collective-permute-start(f32[16,512]{1,0:T(8,128)S(1)} %multiply_add_fusion.2), channel_id=1, source_target_pairs={{0,8},{8,16},{16,24},{24,32},{32,40},{40,48},{48,56},{56,64},{64,7... | collective-permute-start | bytes 98312 | tf_op jit(solution)/shard_map/while/body/eval_jaxpr/ppermute | solution.py:10
  459.1 9.1 %collective-permute-start = (f32[16,512]{1,0:T(8,128)S(1)}, f32[16,512]{1,0:T(8,128)S(1)}, u32[]{:S(2)}, u32[]{:S(2)}) collective-permute-start(f32[16,512]{1,0:T(8,128)S(1)} %multiply_add_fusion.2), channel_id=1, source_target_pairs={{0,8},{8,16},{16,24},{24,32},{32,40},{40,48},{48,56},{56,64},{64,7... | collective-permute-start | bytes 98312 | tf_op jit(solution)/shard_map/while/body/eval_jaxpr/ppermute | solution.py:10
  468.2 9.1 %collective-permute-start = (f32[16,512]{1,0:T(8,128)S(1)}, f32[16,512]{1,0:T(8,128)S(1)}, u32[]{:S(2)}, u32[]{:S(2)}) collective-permute-start(f32[16,512]{1,0:T(8,128)S(1)} %multiply_add_fusion.2), channel_id=1, source_target_pairs={{0,8},{8,16},{16,24},{24,32},{32,40},{40,48},{48,56},{56,64},{64,7... | collective-permute-start | bytes 98312 | tf_op jit(solution)/shard_map/while/body/eval_jaxpr/ppermute | solution.py:10
  477.3 9.1 %collective-permute-start = (f32[16,512]{1,0:T(8,128)S(1)}, f32[16,512]{1,0:T(8,128)S(1)}, u32[]{:S(2)}, u32[]{:S(2)}) collective-permute-start(f32[16,512]{1,0:T(8,128)S(1)} %multiply_add_fusion.2), channel_id=1, source_target_pairs={{0,8},{8,16},{16,24},{24,32},{32,40},{40,48},{48,56},{56,64},{64,7... | collective-permute-start | bytes 98312 | tf_op jit(solution)/shard_map/while/body/eval_jaxpr/ppermute | solution.py:10
  486.5 9.1 %collective-permute-start = (f32[16,512]{1,0:T(8,128)S(1)}, f32[16,512]{1,0:T(8,128)S(1)}, u32[]{:S(2)}, u32[]{:S(2)}) collective-permute-start(f32[16,512]{1,0:T(8,128)S(1)} %multiply_add_fusion.2), channel_id=1, source_target_pairs={{0,8},{8,16},{16,24},{24,32},{32,40},{40,48},{48,56},{56,64},{64,7... | collective-permute-start | bytes 98312 | tf_op jit(solution)/shard_map/while/body/eval_jaxpr/ppermute | solution.py:10
  495.6 9.2 %collective-permute-start = (f32[16,512]{1,0:T(8,128)S(1)}, f32[16,512]{1,0:T(8,128)S(1)}, u32[]{:S(2)}, u32[]{:S(2)}) collective-permute-start(f32[16,512]{1,0:T(8,128)S(1)} %multiply_add_fusion.2), channel_id=1, source_target_pairs={{0,8},{8,16},{16,24},{24,32},{32,40},{40,48},{48,56},{56,64},{64,7... | collective-permute-start | bytes 98312 | tf_op jit(solution)/shard_map/while/body/eval_jaxpr/ppermute | solution.py:10
  504.9 9.1 %collective-permute-start = (f32[16,512]{1,0:T(8,128)S(1)}, f32[16,512]{1,0:T(8,128)S(1)}, u32[]{:S(2)}, u32[]{:S(2)}) collective-permute-start(f32[16,512]{1,0:T(8,128)S(1)} %multiply_add_fusion.2), channel_id=1, source_target_pairs={{0,8},{8,16},{16,24},{24,32},{32,40},{40,48},{48,56},{56,64},{64,7... | collective-permute-start | bytes 98312 | tf_op jit(solution)/shard_map/while/body/eval_jaxpr/ppermute | solution.py:10
  514.0 9.1 %collective-permute-start = (f32[16,512]{1,0:T(8,128)S(1)}, f32[16,512]{1,0:T(8,128)S(1)}, u32[]{:S(2)}, u32[]{:S(2)}) collective-permute-start(f32[16,512]{1,0:T(8,128)S(1)} %multiply_add_fusion.2), channel_id=1, source_target_pairs={{0,8},{8,16},{16,24},{24,32},{32,40},{40,48},{48,56},{56,64},{64,7... | collective-permute-start | bytes 98312 | tf_op jit(solution)/shard_map/while/body/eval_jaxpr/ppermute | solution.py:10
  523.1 9.1 %collective-permute-start = (f32[16,512]{1,0:T(8,128)S(1)}, f32[16,512]{1,0:T(8,128)S(1)}, u32[]{:S(2)}, u32[]{:S(2)}) collective-permute-start(f32[16,512]{1,0:T(8,128)S(1)} %multiply_add_fusion.2), channel_id=1, source_target_pairs={{0,8},{8,16},{16,24},{24,32},{32,40},{40,48},{48,56},{56,64},{64,7... | collective-permute-start | bytes 98312 | tf_op jit(solution)/shard_map/while/body/eval_jaxpr/ppermute | solution.py:10
  532.3 9.1 %collective-permute-start = (f32[16,512]{1,0:T(8,128)S(1)}, f32[16,512]{1,0:T(8,128)S(1)}, u32[]{:S(2)}, u32[]{:S(2)}) collective-permute-start(f32[16,512]{1,0:T(8,128)S(1)} %multiply_add_fusion.2), channel_id=1, source_target_pairs={{0,8},{8,16},{16,24},{24,32},{32,40},{40,48},{48,56},{56,64},{64,7... | collective-permute-start | bytes 98312 | tf_op jit(solution)/shard_map/while/body/eval_jaxpr/ppermute | solution.py:10
  541.4 9.1 %collective-permute-start = (f32[16,512]{1,0:T(8,128)S(1)}, f32[16,512]{1,0:T(8,128)S(1)}, u32[]{:S(2)}, u32[]{:S(2)}) collective-permute-start(f32[16,512]{1,0:T(8,128)S(1)} %multiply_add_fusion.2), channel_id=1, source_target_pairs={{0,8},{8,16},{16,24},{24,32},{32,40},{40,48},{48,56},{56,64},{64,7... | collective-permute-start | bytes 98312 | tf_op jit(solution)/shard_map/while/body/eval_jaxpr/ppermute | solution.py:10
  550.6 9.1 %collective-permute-start = (f32[16,512]{1,0:T(8,128)S(1)}, f32[16,512]{1,0:T(8,128)S(1)}, u32[]{:S(2)}, u32[]{:S(2)}) collective-permute-start(f32[16,512]{1,0:T(8,128)S(1)} %multiply_add_fusion.2), channel_id=1, source_target_pairs={{0,8},{8,16},{16,24},{24,32},{32,40},{40,48},{48,56},{56,64},{64,7... | collective-permute-start | bytes 98312 | tf_op jit(solution)/shard_map/while/body/eval_jaxpr/ppermute | solution.py:10
  559.7 9.2 %collective-permute-start = (f32[16,512]{1,0:T(8,128)S(1)}, f32[16,512]{1,0:T(8,128)S(1)}, u32[]{:S(2)}, u32[]{:S(2)}) collective-permute-start(f32[16,512]{1,0:T(8,128)S(1)} %multiply_add_fusion.2), channel_id=1, source_target_pairs={{0,8},{8,16},{16,24},{24,32},{32,40},{40,48},{48,56},{56,64},{64,7... | collective-permute-start | bytes 98312 | tf_op jit(solution)/shard_map/while/body/eval_jaxpr/ppermute | solution.py:10
  569.0 9.1 %collective-permute-start = (f32[16,512]{1,0:T(8,128)S(1)}, f32[16,512]{1,0:T(8,128)S(1)}, u32[]{:S(2)}, u32[]{:S(2)}) collective-permute-start(f32[16,512]{1,0:T(8,128)S(1)} %multiply_add_fusion.2), channel_id=1, source_target_pairs={{0,8},{8,16},{16,24},{24,32},{32,40},{40,48},{48,56},{56,64},{64,7... | collective-permute-start | bytes 98312 | tf_op jit(solution)/shard_map/while/body/eval_jaxpr/ppermute | solution.py:10
  578.1 9.1 %collective-permute-start = (f32[16,512]{1,0:T(8,128)S(1)}, f32[16,512]{1,0:T(8,128)S(1)}, u32[]{:S(2)}, u32[]{:S(2)}) collective-permute-start(f32[16,512]{1,0:T(8,128)S(1)} %multiply_add_fusion.2), channel_id=1, source_target_pairs={{0,8},{8,16},{16,24},{24,32},{32,40},{40,48},{48,56},{56,64},{64,7... | collective-permute-start | bytes 98312 | tf_op jit(solution)/shard_map/while/body/eval_jaxpr/ppermute | solution.py:10
  587.2 9.1 %collective-permute-start = (f32[16,512]{1,0:T(8,128)S(1)}, f32[16,512]{1,0:T(8,128)S(1)}, u32[]{:S(2)}, u32[]{:S(2)}) collective-permute-start(f32[16,512]{1,0:T(8,128)S(1)} %multiply_add_fusion.2), channel_id=1, source_target_pairs={{0,8},{8,16},{16,24},{24,32},{32,40},{40,48},{48,56},{56,64},{64,7... | collective-permute-start | bytes 98312 | tf_op jit(solution)/shard_map/while/body/eval_jaxpr/ppermute | solution.py:10
  596.4 9.1 %collective-permute-start = (f32[16,512]{1,0:T(8,128)S(1)}, f32[16,512]{1,0:T(8,128)S(1)}, u32[]{:S(2)}, u32[]{:S(2)}) collective-permute-start(f32[16,512]{1,0:T(8,128)S(1)} %multiply_add_fusion.2), channel_id=1, source_target_pairs={{0,8},{8,16},{16,24},{24,32},{32,40},{40,48},{48,56},{56,64},{64,7... | collective-permute-start | bytes 98312 | tf_op jit(solution)/shard_map/while/body/eval_jaxpr/ppermute | solution.py:10
  605.5 9.1 %collective-permute-start = (f32[16,512]{1,0:T(8,128)S(1)}, f32[16,512]{1,0:T(8,128)S(1)}, u32[]{:S(2)}, u32[]{:S(2)}) collective-permute-start(f32[16,512]{1,0:T(8,128)S(1)} %multiply_add_fusion.2), channel_id=1, source_target_pairs={{0,8},{8,16},{16,24},{24,32},{32,40},{40,48},{48,56},{56,64},{64,7... | collective-permute-start | bytes 98312 | tf_op jit(solution)/shard_map/while/body/eval_jaxpr/ppermute | solution.py:10
  614.7 9.1 %collective-permute-start = (f32[16,512]{1,0:T(8,128)S(1)}, f32[16,512]{1,0:T(8,128)S(1)}, u32[]{:S(2)}, u32[]{:S(2)}) collective-permute-start(f32[16,512]{1,0:T(8,128)S(1)} %multiply_add_fusion.2), channel_id=1, source_target_pairs={{0,8},{8,16},{16,24},{24,32},{32,40},{40,48},{48,56},{56,64},{64,7... | collective-permute-start | bytes 98312 | tf_op jit(solution)/shard_map/while/body/eval_jaxpr/ppermute | solution.py:10
  623.8 9.1 %collective-permute-start = (f32[16,512]{1,0:T(8,128)S(1)}, f32[16,512]{1,0:T(8,128)S(1)}, u32[]{:S(2)}, u32[]{:S(2)}) collective-permute-start(f32[16,512]{1,0:T(8,128)S(1)} %multiply_add_fusion.2), channel_id=1, source_target_pairs={{0,8},{8,16},{16,24},{24,32},{32,40},{40,48},{48,56},{56,64},{64,7... | collective-permute-start | bytes 98312 | tf_op jit(solution)/shard_map/while/body/eval_jaxpr/ppermute | solution.py:10
  632.9 9.1 %collective-permute-start = (f32[16,512]{1,0:T(8,128)S(1)}, f32[16,512]{1,0:T(8,128)S(1)}, u32[]{:S(2)}, u32[]{:S(2)}) collective-permute-start(f32[16,512]{1,0:T(8,128)S(1)} %multiply_add_fusion.2), channel_id=1, source_target_pairs={{0,8},{8,16},{16,24},{24,32},{32,40},{40,48},{48,56},{56,64},{64,7... | collective-permute-start | bytes 98312 | tf_op jit(solution)/shard_map/while/body/eval_jaxpr/ppermute | solution.py:10
  (16 other events, 110.2 us)
where the time goes:
time: 688 us; the launch traced here: 685 us
  waiting for transfers between devices  455 us (66%)
  starting transfers between devices  132 us (19%)
  matrix products  47.8 us (7%)
  local copies, waits for them, and re-layouts  22.5 us (3%)
  blocking collectives  14.7 us (2%)
  other arithmetic  10.9 us (2%)
    ppermute x66, waiting for transfers between devices, passed_along(): return lax.ppermute(array, axis, pairs)  455 us
    ppermute x66, starting transfers between devices, passed_along(): return lax.ppermute(array, axis, pairs)  132 us
    conv_general_dilated x8, matrix products, depthwise(): lax.conv_general_dilated(extended, jnp.flip(kernel, 0)[:, None, :], (1,),...  27.7 us
    psum x1, blocking collectives, local(): squares = lax.psum(jnp.sum(embedded * embedded, axis=1), 'ch')  14.7 us
  transfers between devices with their start and end apart: 66, of which 64 were waited for; matrix products, arithmetic and copies ran while one was open for 3% of the time, Pallas kernels for 0%

commit v1 on v0

v1 whole, which is shorter than its diff:
```python
import functools

import jax
import jax.numpy as jnp
import ml_dtypes
import numpy as np
from jax import lax
from jax.experimental import pallas as pl
from jax.experimental.pallas import tpu as pltpu
from jax.sharding import PartitionSpec as P

F32 = jnp.float32
BF16 = jnp.bfloat16
LANES = 128
STEPS = 64
LINES = 8
HALO_STEPS = 18
SPAN = 6
EXT_STEPS = SPAN + HALO_STEPS + SPAN + STEPS
OUT_STEPS = EXT_STEPS - SPAN
HALO_IDS = 256
BLOCK = 16
SECOND_ROWS = (SPAN + STEPS) * LINES
FREQS = 672
INNER = 8
NT = (((1,), (1,)), ((), ()))


def step_times():
    lines = np.arange(LINES)
    halo = -HALO_STEPS * LINES + lines[None] * HALO_STEPS + np.arange(-SPAN, HALO_STEPS)[:, None]
    main = lines[None] * STEPS + np.arange(-SPAN, STEPS)[:, None]
    return np.concatenate([halo, main], 0)


def tables(taps):
    times = step_times()
    pair = np.arange(FREQS)
    freq = (pair // 16) * 8 + pair % 8 + 0.5
    quarter = np.where(pair % 16 < 8, 0.0, 0.25)
    origin = HALO_STEPS * LINES

    def wave(position):
        return np.cos(2 * np.pi * (np.outer(freq, position) / FREQS + quarter[:, None]))

    used = times[SPAN:].copy()
    valid = np.ones(used.shape, bool)
    valid[HALO_STEPS : HALO_STEPS + SPAN] = False
    valid &= used >= -(taps - 1 + SPAN)
    forward = wave((used + origin).reshape(-1)) * valid.reshape(1, -1)
    taps_wave = wave(np.arange(taps))
    halo_rows = times[SPAN + HALO_STEPS - SPAN : SPAN + HALO_STEPS].reshape(-1)
    main_rows = times[SPAN + HALO_STEPS + SPAN :].reshape(-1)
    back = wave(np.concatenate([halo_rows, main_rows]) + origin).T * (2.0 / FREQS)
    order = np.zeros((STEPS * LINES, STEPS * LINES), np.float32)
    order[main_rows, np.arange(main_rows.size)] = 1.0
    half = lambda a: np.asarray(a, np.float32).astype(ml_dtypes.bfloat16)
    return dict(
        forward=half(forward),
        taps_wave=split_wave(taps_wave),
        back=half(back),
        order=half(order),
    )


def split_wave(wave):
    high = np.asarray(wave, np.float32).astype(ml_dtypes.bfloat16)
    low = (wave - high.astype(np.float64)).astype(ml_dtypes.bfloat16)
    return np.concatenate([high, low, high], 1)


def lanes_of(group):
    return slice(group * LANES, (group + 1) * LANES)


def halves(values):
    high = values.astype(BF16)
    return high, (values - high.astype(F32)).astype(BF16)


def square_sums(table_ref, sums_ref):
    table = table_ref[...].astype(F32)
    high, low = halves(table * table)
    ones = jnp.ones((8, table.shape[1]), BF16)
    total = lax.dot_general(ones, high, NT, preferred_element_type=F32)
    total += lax.dot_general(ones, low, NT, preferred_element_type=F32)
    sums_ref[...] = jnp.broadcast_to(total[None, :1], sums_ref.shape)


def spectrum_of(wave_ref, medium_ref, spectrum_ref):
    high, low = halves(medium_ref[...])
    spectrum_ref[...] = jnp.dot(
        wave_ref[...], jnp.concatenate([high, high, low], 0), preferred_element_type=F32
    )


def one_hot(place, before, own, vocab):
    def digits(ids):
        high = lax.shift_right_arithmetic(ids, 4)
        low = ids - high * 16
        row = lax.broadcasted_iota(jnp.int32, (8, ids.shape[1]), 0)
        return jnp.where(row == 0, high, jnp.where(row == 1, low, 0)).astype(F32).astype(BF16)

    def picked(ids, first, steps, spread, shift):
        rows = steps * LINES
        row = lax.broadcasted_iota(jnp.int32, (rows, 1), 0)
        step = lax.shift_right_logical(row, 3)
        time = lax.bitwise_and(row, LINES - 1) * spread + step + shift
        column = lax.broadcasted_iota(jnp.int32, (rows, ids.shape[1]), 1) + first
        pick = jnp.where(column == time, 1.0, 0.0).astype(BF16)
        return lax.dot_general(pick, digits(ids), NT, preferred_element_type=F32)

    before = jnp.where(place > 0, before, -1)
    halo = picked(before, -HALO_IDS, SPAN + HALO_STEPS, HALO_STEPS, -LINES * HALO_STEPS - SPAN)
    edge = picked(before, -HALO_IDS, SPAN, STEPS, -SPAN)
    main = picked(own, 0, SPAN + STEPS, STEPS, -SPAN)
    column = jnp.concatenate([halo, edge + main[: SPAN * LINES], main[SPAN * LINES :]], 0)
    ids = (column[:, 0:1] * 16.0 + column[:, 1:2]).astype(jnp.int32)
    hot = ids == lax.broadcasted_iota(jnp.int32, (column.shape[0], vocab), 1)
    return jnp.where(hot, 1.0, 0.0).astype(BF16)


def taps_of(filters_ref, block, stream, group):
    return [
        jnp.broadcast_to(filters_ref[block, stream, d : d + 1, lanes_of(group)], (LINES, LANES))
        for d in range(SPAN + 1)
    ]


def tapped(window, taps, rows):
    total = None
    for d, tap in enumerate(taps):
        term = window[SPAN - d : SPAN - d + rows] * tap[None]
        total = term if total is None else total + term
    return total


def rows_at(start, size):
    return pl.ds(start if isinstance(start, int) else pl.multiple_of(start, 16), size)


def second_window(second_ref, b, group):
    rows = rows_at(b * BLOCK * LINES, (BLOCK + SPAN) * LINES)
    return second_ref[rows, lanes_of(group)].astype(F32).reshape(BLOCK + SPAN, LINES, LANES)


def driven_steps(driven_ref, b, group):
    rows = rows_at(b * BLOCK * LINES, BLOCK * LINES)
    return driven_ref[rows, lanes_of(group)].astype(F32).reshape(BLOCK, LINES, LANES)


def parts_of(kept_ref, modes):
    return (
        kept_ref.at[pl.ds(0, SECOND_ROWS)],
        kept_ref.at[pl.ds(SECOND_ROWS, STEPS * LINES)],
        kept_ref.at[pl.ds(SECOND_ROWS + STEPS * LINES, 2 * modes * LINES)],
    )


class Stage:
    def __init__(self, width, modes, kept_ref, ext_ref, gated_ref, query_ref, mixed_ref):
        self.width, self.modes = width, modes
        self.count = width // LANES
        self.second, self.driven, self.endings = parts_of(kept_ref, modes)
        self.ext, self.gated, self.query, self.mixed = ext_ref, gated_ref, query_ref, mixed_ref

    def embed(self, hot, scaled):
        rows = jnp.dot(hot, scaled, preferred_element_type=F32)
        self.ext[...] = rows.reshape(EXT_STEPS, LINES, self.width)

    def gate(self, filters_ref, at, steps):
        for g in range(self.count):
            window = self.ext[pl.ds(at, steps + SPAN), :, lanes_of(g)]
            key, value = [
                tapped(window, taps_of(filters_ref, 0, s, g), steps)
                for s in (1, 2)
            ]
            self.gated[rows_at(at * LINES, steps * LINES), lanes_of(g)] = (
                (key * value).reshape(steps * LINES, LANES).astype(BF16)
            )

    def ask(self, filters_ref, at, steps):
        for g in range(self.count):
            window = self.ext[pl.ds(at, steps + SPAN), :, lanes_of(g)]
            taps = taps_of(filters_ref, 0, 0, g)
            self.query[pl.ds(at, steps), :, lanes_of(g)] = tapped(window, taps, steps)

    def edges(self, filters_ref):
        gap = slice(HALO_STEPS * LINES, (HALO_STEPS + SPAN) * LINES)
        self.gated[gap, :] = jnp.zeros((SPAN * LINES, self.width), BF16)
        self.gate(filters_ref, 0, HALO_STEPS)
        self.ask(filters_ref, HALO_STEPS - SPAN, SPAN)

    def forward(self, forward_ref, spectrum_ref):
        wave = jnp.dot(forward_ref[...], self.gated[...], preferred_element_type=F32)
        wave = wave.reshape(FREQS // 16, 16, self.width)
        shape = spectrum_ref[...].reshape(FREQS // 16, 16, self.width)
        real, imag = wave[:, :8], wave[:, 8:]
        real_h, imag_h = shape[:, :8], shape[:, 8:]
        product = jnp.concatenate(
            [real * real_h - imag * imag_h, real * imag_h + imag * real_h], axis=1
        )
        self.mixed[...] = product.reshape(FREQS, self.width).astype(BF16)

    def backward(self, back_ref):
        middle = jnp.dot(back_ref[...], self.mixed[...], preferred_element_type=F32)
        middle = middle.reshape(SPAN + STEPS, LINES, self.width)
        halo = middle[:SPAN] * self.query[HALO_STEPS - SPAN : HALO_STEPS]
        halo = halo.astype(BF16).astype(F32)
        main = middle[SPAN:] * self.query[HALO_STEPS + SPAN :]
        main = main.reshape(STEPS * LINES, self.width).astype(BF16)
        self.second[SPAN * LINES :, :] = main
        last = main[(STEPS - SPAN) * LINES :].astype(F32).reshape(SPAN, LINES, self.width)
        first = []
        for k in range(SPAN):
            own = pltpu.roll(last[k], 1, 0)
            other = pltpu.roll(halo[k], 1, 0)
            line = lax.broadcasted_iota(jnp.int32, own.shape, 0)
            first.append(jnp.where(line == 0, other, own))
        self.second[: SPAN * LINES, :] = jnp.concatenate(first, 0).astype(BF16)

    def drive(self, filters_ref, b):
        for g in range(self.count):
            window = second_window(self.second, b, g)
            key, value = [
                tapped(window, taps_of(filters_ref, 1, s, g), BLOCK)
                for s in (1, 2)
            ]
            self.driven[rows_at(b * BLOCK * LINES, BLOCK * LINES), lanes_of(g)] = (
                (key * value).reshape(BLOCK * LINES, LANES).astype(BF16)
            )

    def decays(self, rates_ref, g):
        lanes = lanes_of(g)
        return [
            jnp.exp(-jnp.broadcast_to(rates_ref[r : r + 1, lanes], (LINES, LANES)))
            for r in range(self.modes)
        ]

    def absorb(self, decays, states, b, g):
        values = driven_steps(self.driven, b, g)
        for k in range(BLOCK):
            states = tuple(d * s + values[k] for d, s in zip(decays, states))
        return states

    def settle(self, rates_ref, state_ref, states, g):
        lanes = lanes_of(g)
        line = lax.broadcasted_iota(jnp.int32, (LINES, LANES), 0).astype(F32)
        for r in range(self.modes):
            self.endings[r * 2 * LINES : (r + 1) * 2 * LINES, lanes_of(g)] = jnp.concatenate(
                [h.astype(F32) for h in halves(states[r])], 0
            ).astype(BF16)
            weight = jnp.exp(-rates_ref[r : r + 1, lanes] * ((LINES - 1.0 - line) * STEPS))
            ending = jnp.sum(states[r] * weight, axis=0, keepdims=True).astype(state_ref.dtype)
            state_ref[0, r : r + 1, lanes] = ending


def first_part(
    channels,
    place_ref,
    squares_ref,
    before_ref,
    ids_ref,
    table_ref,
    gain_ref,
    filters_ref,
    rates_ref,
    forward_ref,
    spectrum_ref,
    back_ref,
    state_ref,
    kept_ref,
    ext_ref,
    gated_ref,
    query_ref,
    mixed_ref,
    forward_v,
    back_v,
    sems,
):
    loads = [
        pltpu.make_async_copy(forward_ref, forward_v, sems.at[0]),
        pltpu.make_async_copy(back_ref, back_v, sems.at[1]),
    ]
    for load in loads:
        load.start()
    vocab, width = table_ref.shape
    modes = rates_ref.shape[0]
    stage = Stage(width, modes, kept_ref, ext_ref, gated_ref, query_ref, mixed_ref)
    before = before_ref[:, before_ref.shape[1] - HALO_IDS :]
    hot = one_hot(place_ref[0], before, ids_ref[...], vocab)
    inverse = lax.rsqrt(jnp.sum(squares_ref[...], axis=0) / channels + 1e-06)
    column = jnp.transpose(jnp.broadcast_to(inverse, (8, vocab)))[:, 0:1]
    scaled = (table_ref[...].astype(F32) * column * gain_ref[...]).astype(BF16)
    main = HALO_STEPS + SPAN

    def loop(body):
        def step(i, carry):
            body(i)
            return carry

        lax.fori_loop(0, STEPS // BLOCK, step, 0)

    stage.embed(hot, scaled)
    stage.edges(filters_ref)

    def convolve(i):
        stage.gate(filters_ref, main + i * BLOCK, BLOCK)
        stage.ask(filters_ref, main + i * BLOCK, BLOCK)

    loop(convolve)
    loads[0].wait()
    stage.forward(forward_v, spectrum_ref)
    loads[1].wait()
    stage.backward(back_v)
    loop(lambda i: stage.drive(filters_ref, i))
    zero = jnp.zeros((LINES, LANES), F32)
    for g in range(stage.count):
        decays = stage.decays(rates_ref, g)

        def gather(i, states, g=g, decays=decays):
            return stage.absorb(decays, states, i, g)

        states = lax.fori_loop(0, STEPS // BLOCK, gather, (zero,) * modes)
        stage.settle(rates_ref, state_ref, states, g)
    for k in range(1, state_ref.shape[0]):
        state_ref[k] = state_ref[0]


def coefficients(rates, residues):
    double = 2.0 * rates
    series = double * (1.0 + double * (-0.5 + double * (1.0 / 6 + double * (-1.0 / 24))))
    return residues * jnp.sqrt(jnp.where(double < 0.02, series, 1.0 - jnp.exp(-double)))


def near_part(place_ref, rows_ref, rates_ref, near_ref, total_ref):
    across = jnp.exp(-rates_ref[...] * (1.0 * STEPS * LINES))
    own = lax.rem(place_ref[0], rows_ref.shape[0])
    total = jnp.zeros(rates_ref.shape, F32)
    near = total
    for j in range(rows_ref.shape[0]):
        near = jnp.where(own == j, total, near)
        total = across * total + rows_ref[j].astype(F32)
    near_ref[...] = near
    total_ref[...] = jnp.broadcast_to(total.astype(BF16)[None], total_ref.shape)


def second_part(
    filters_ref,
    rates_ref,
    residues_ref,
    kept_ref,
    order_ref,
    query_ref,
    whole_ref,
    weights_ref,
    query_v,
    whole_v,
    order_v,
    sems,
):
    load = pltpu.make_async_copy(order_ref, order_v, sems.at[0])
    load.start()
    weights_ref[...] = coefficients(rates_ref[...], residues_ref[...])
    modes, width = rates_ref.shape
    groups = width // LANES
    index = lax.broadcasted_iota(jnp.int32, (LINES, LANES), 0)
    second_ref, driven_ref, endings_ref = parts_of(kept_ref, modes)
    for group in range(groups):
        taps = taps_of(filters_ref, 1, 0, group)

        def conv_query(b, carry, group=group, taps=taps):
            window = second_window(second_ref, b, group)
            rows = pl.ds(pl.multiple_of(b * BLOCK * LINES, BLOCK * LINES), BLOCK * LINES)
            query_v[rows, lanes_of(group)] = (
                tapped(window, taps, BLOCK).reshape(BLOCK * LINES, LANES).astype(BF16)
            )
            return carry

        lax.fori_loop(0, STEPS // BLOCK, conv_query, 0)

        decays, weights, starts = [], [], []
        for r in range(modes):
            rate = jnp.broadcast_to(rates_ref[r : r + 1, lanes_of(group)], (LINES, LANES))
            ending = endings_ref[r * 2 * LINES : (r + 1) * 2 * LINES, lanes_of(group)].astype(F32)
            total = ending[:LINES] + ending[LINES:]
            for k in (1, 2, 4):
                moved = jnp.where(index >= k, pltpu.roll(total, k, 0), 0.0)
                total = total + jnp.exp(-rate * (1.0 * STEPS * k)) * moved
            starts.append(jnp.where(index >= 1, pltpu.roll(total, 1, 0), 0.0))
            decays.append(jnp.exp(-rate))
            weights.append(
                jnp.broadcast_to(weights_ref[r : r + 1, lanes_of(group)], (LINES, LANES))
            )

        def respond(b, states, group=group, decays=decays, weights=weights):
            values = driven_steps(driven_ref, b, group)
            outs = []
            for k in range(BLOCK):
                states = tuple(d * s + values[k] for d, s in zip(decays, states))
                sums = [w * s for w, s in zip(weights, states)]
                while len(sums) > 1:
                    sums = [a + b for a, b in zip(sums[0::2], sums[1::2])]
                outs.append(sums[0])
            rows = pl.ds(pl.multiple_of(b * BLOCK * LINES, BLOCK * LINES), BLOCK * LINES)
            whole_v[rows, lanes_of(group)] = jnp.concatenate(outs, 0)
            return states

        lax.fori_loop(0, STEPS // BLOCK, respond, tuple(starts))
    load.wait()
    query_ref[...] = jnp.dot(
        order_v[...], query_v[...], preferred_element_type=F32
    ).astype(BF16)
    high, low = halves(whole_v[...])
    whole_ref[...] = jnp.dot(order_v[...], high, preferred_element_type=F32) + jnp.dot(
        order_v[...], low, preferred_element_type=F32
    )


def third_part(
    inner,
    place_ref,
    near_ref,
    totals_ref,
    rates_ref,
    weights_ref,
    query_ref,
    whole_ref,
    out_ref,
    result_v,
    sems,
):
    modes, width = rates_ref.shape
    groups = width // LANES
    span = 1.0 * STEPS * LINES
    across = jnp.exp(-rates_ref[...] * (span * inner))
    own = lax.rem(place_ref[0], inner)
    rank = lax.div(place_ref[0], inner)
    far = jnp.zeros(rates_ref.shape, F32)
    for j in range(totals_ref.shape[0]):
        far = jnp.where(j < rank, across * far + totals_ref[j].astype(F32), far)
    incoming = near_ref[...] + jnp.exp(-rates_ref[...] * (span * own.astype(F32))) * far

    stores = []
    across = jnp.exp(-rates_ref[...] * LINES)
    entering = weights_ref[...] * incoming
    line = lax.broadcasted_iota(jnp.int32, (LINES, LANES), 0).astype(F32)
    for group in range(groups):
        decays, terms = [], []
        for r in range(modes):
            decays.append(jnp.broadcast_to(across[r : r + 1, lanes_of(group)], (LINES, LANES)))
            rise = jnp.exp(-rates_ref[r : r + 1, lanes_of(group)] * (line + 1.0))
            terms.append(rise * entering[r : r + 1, lanes_of(group)])

        def lift(b, terms, group=group, decays=decays):
            rows = pl.ds(pl.multiple_of(b * 64, 64), 64)
            outs = []
            for k in range(8):
                sums = list(terms)
                while len(sums) > 1:
                    sums = [a + b for a, b in zip(sums[0::2], sums[1::2])]
                outs.append(sums[0])
                terms = tuple(t * d for t, d in zip(terms, decays))
            whole = whole_ref[rows, lanes_of(group)] + jnp.concatenate(outs, 0)
            query = query_ref[rows, lanes_of(group)].astype(F32)
            result_v[rows, lanes_of(group)] = (query * whole).astype(BF16)
            return terms

        lax.fori_loop(0, STEPS // 8, lift, tuple(terms))
        stores.append(
            pltpu.make_async_copy(
                result_v.at[:, lanes_of(group)], out_ref.at[:, lanes_of(group)], sems.at[group]
            )
        )
        stores[-1].start()
    for store in stores:
        store.wait()


VMEM = pl.BlockSpec(memory_space=pltpu.VMEM)
SMEM = pl.BlockSpec(memory_space=pltpu.SMEM)
HBM = pl.BlockSpec(memory_space=pl.ANY)


FAR = pl.BlockSpec(memory_space=pltpu.HBM)


def far(array):
    return pltpu.with_memory_space_constraint(jnp.asarray(array), pltpu.HBM)


def cost(flops, moved):
    return pl.CostEstimate(flops=int(flops), bytes_accessed=int(moved), transcendentals=0)


def call(
    kernel, name, ins, outs, scratch=(), sems=0, out_space=None, limit=24, flops=1e9, moved=4e6
):
    return pl.pallas_call(
        kernel,
        name=name,
        in_specs=ins,
        out_specs=[out_space or VMEM] * len(outs),
        out_shape=[jax.ShapeDtypeStruct(*o) for o in outs],
        scratch_shapes=[pltpu.VMEM(*s) for s in scratch]
        + ([pltpu.SemaphoreType.DMA((sems,))] if sems else []),
        compiler_params=pltpu.CompilerParams(vmem_limit_bytes=limit << 20),
        cost_estimate=cost(flops, moved),
    )


def local(
    token_ids, embed_table, norm_gain, short_filters, medium_filter, mode_rates, mode_residues
):
    vocab, width = embed_table.shape
    count = token_ids.shape[0]
    modes = mode_rates.shape[0]
    taps = medium_filter.shape[0]
    shards = lax.axis_size("ch")
    length = lax.axis_size("seq")
    inner = min(INNER, length)
    near_groups = [[o * inner + i for i in range(inner)] for o in range(length // inner)]
    far_groups = [[o * inner + i for o in range(length // inner)] for i in range(inner)]
    const = tables(taps)
    place = jnp.reshape(lax.axis_index("seq").astype(jnp.int32), (1,))

    before = lax.ppermute(token_ids, "seq", [(i, i + 1) for i in range(length - 1)])
    (partial,) = call(
        square_sums, "square_sums", [VMEM], [((shards, 1, vocab), F32)], limit=8
    )(embed_table)
    squares = lax.all_to_all(partial, "ch", 0, 0)
    (spectrum,) = call(
        spectrum_of, "spectrum_of", [VMEM] * 2, [((FREQS, width), F32)], limit=8
    )(const["taps_wave"], medium_filter)
    kept_shape = (SECOND_ROWS + STEPS * LINES + 2 * modes * LINES, width)
    state, kept = call(
        functools.partial(first_part, channels_of(width, shards)),
        "first_part",
        [SMEM] + [VMEM] * 7 + [FAR, VMEM, FAR],
        [((inner, modes, width), BF16), (kept_shape, BF16)],
        [
            ((EXT_STEPS, LINES, width), F32),
            ((OUT_STEPS * LINES, width), BF16),
            ((OUT_STEPS, LINES, width), F32),
            ((FREQS, width), BF16),
            (const["forward"].shape, BF16),
            (const["back"].shape, BF16),
        ],
        sems=2,
    )(
        place,
        squares,
        before[None],
        token_ids[None],
        embed_table,
        norm_gain[None],
        short_filters,
        mode_rates,
        far(const["forward"]),
        spectrum,
        far(const["back"]),
    )
    rows = lax.all_to_all(state, "seq", 0, 0, axis_index_groups=near_groups, tiled=True)
    query, whole, weights = call(
        second_part,
        "second_part",
        [VMEM] * 4 + [FAR],
        [((count, width), BF16), ((count, width), F32), ((modes, width), F32)],
        [((count, width), BF16), ((count, width), F32), ((count, count), BF16)],
        sems=1,
        flops=4e9,
        moved=1e7,
    )(short_filters, mode_rates, mode_residues, kept, far(const["order"]))
    near, totals = call(
        near_part,
        "near_part",
        [SMEM] + [VMEM] * 2,
        [((modes, width), F32), ((length // inner, modes, width), BF16)],
        limit=4,
    )(place, rows, mode_rates)
    totals = lax.all_to_all(totals, "seq", 0, 0, axis_index_groups=far_groups, tiled=True)
    (out,) = call(
        functools.partial(third_part, inner),
        "third_part",
        [SMEM] + [VMEM] * 6,
        [((count, width), BF16)],
        [((count, width), BF16)],
        sems=width // LANES,
        out_space=HBM,
        limit=12,
    )(place, near, totals, mode_rates, weights, query, whole)
    return out


def channels_of(width, shards):
    return width * shards


def solution(mesh):
    placed = (
        P("seq"),
        P(None, "ch"),
        P("ch"),
        P(None, None, None, "ch"),
        P(None, "ch"),
        P(None, "ch"),
        P(None, "ch"),
    )
    return jax.shard_map(
        local, mesh=mesh, in_specs=placed, out_specs=P("seq", "ch"), check_vma=False
    )
```

time: 688 us -> 59.1 us (0.09)
  the two profiles are of different devices: /device:TPU:256 before, /device:TPU:2 now
where the time goes in v1:
time: 59.1 us; the launch traced here: 58.8 us
  starting transfers between devices  20.9 us (35%)
  Pallas kernels  15.4 us (26%)
  blocking collectives  14.6 us (25%)
  waiting for transfers between devices  6.73 us (11%)
  local copies, waits for them, and re-layouts  1.1 us (2%)
    all_to_all x1, blocking collectives, local(): lax.all_to_all(state, 'seq', 0, 0, axis_index_groups=near_groups, tiled=T...  14.6 us
    all_to_all x1, starting transfers between devices, local(): lax.all_to_all(totals, 'seq', 0, 0, axis_index_groups=far_groups, tiled=T...  10.3 us
    all_to_all x1, starting transfers between devices, local(): squares = lax.all_to_all(partial, 'ch', 0, 0)  9.15 us
    pallas_call x1, Pallas kernels, local(): call(functools.partial(first_part, channels_of(width, shards)), 'first_pa...  6.81 us
    all_to_all x1, waiting for transfers between devices, local(): lax.all_to_all(totals, 'seq', 0, 0, axis_index_groups=far_groups, tiled=T...  4.86 us
    pallas_call x1, Pallas kernels, local(): call(second_part, 'second_part', [VMEM] * 4 + [FAR], [((count, width), BF...  4.21 us
    pallas_call x1, Pallas kernels, local(): call(functools.partial(third_part, inner), 'third_part', [SMEM] + [VMEM]...  2.12 us
    ppermute x1, starting transfers between devices, local(): lax.ppermute(token_ids, 'seq', [(i, i + 1) for i in range(length - 1)])  1.42 us
  transfers between devices with their start and end apart: 3, of which 3 were waited for; matrix products, arithmetic and copies ran while one was open for 0% of the time, Pallas kernels for 8%

profile of v1, /device:TPU:2, one launch (start us, length us, event | category | flops | bytes accessed | tf_op | source)
XLA Modules:
  0.0 58.8 jit_solution(6275297868903615151)
XLA Ops:
  0.0 0.0 copy-start
  0.0 1.0 %copy-done = bf16[512,512]{1,0:T(8,128)(2,1)S(1)} copy-done((bf16[512,512]{1,0:T(8,128)(2,1)S(1)}, bf16[512,512]{1,0:T(8,128)(2,1)}, u32[]{:S(2)}) %copy-start) | copy-done | bytes 524312
  1.0 0.0 copy-start.3
  1.0 0.0 copy-start.5
  1.0 0.0 copy-start.7
  1.0 1.0 %square_sums.1 = f32[8,1,512]{2,1,0:T(1,128)} custom-call(bf16[512,512]{1,0:T(8,128)(2,1)S(1)} %copy-done), custom_call_target="tpu_custom_call" | custom-call | flops 1000000000 | bytes 4000000 | tf_op jit(solution)/shard_map/square_sums/pallas_call | solution.py:528
  2.1 9.2 %all-to-all-start = ((f32[8,1,512]{2,1,0:T(1,128)}), f32[8,1,512]{2,1,0:T(1,128)S(1)}, u32[]{:S(2)}, u32[]{:S(2)}) async-start(f32[8,1,512]{2,1,0:T(1,128)} %square_sums.1), calls=%async_computation | async-start | bytes 32768 | tf_op jit(solution)/shard_map/all_to_all | solution.py:531
  11.2 0.0 copy-done.3
  11.2 0.0 copy-start.8
  11.2 0.0 copy-start.1
  11.3 0.0 copy-start.2
  11.3 0.0 copy-start.4
  11.3 1.4 %collective-permute-start = (s32[512]{0:T(512)S(1)}, s32[512]{0:T(512)S(1)}, u32[]{:S(2)}, u32[]{:S(2)}) collective-permute-start(s32[512]{0:T(512)S(1)} %copy-done.3), channel_id=1, source_target_pairs={{0,8},{8,16},{16,24},{24,32},{32,40},{40,48},{48,56},{56,64},{64,7... | collective-permute-start | bytes 6152 | tf_op jit(solution)/shard_map/ppermute | solution.py:527
  12.7 0.0 copy-done.5
  12.7 0.0 copy-done.7
  12.7 0.5 spectrum_of.1.spectrum_ref
  13.3 0.0 copy-done.8
  13.3 0.7 %collective-permute-done = s32[512]{0:T(512)S(1)} collective-permute-done((s32[512]{0:T(512)S(1)}, s32[512]{0:T(512)S(1)}, u32[]{:S(2)}, u32[]{:S(2)}) %collective-permute-start) | collective-permute-done | bytes 2080 | tf_op jit(solution)/shard_map/ppermute | solution.py:527
  14.0 1.2 %all-to-all-done.squares_ref = f32[8,1,512]{2,1,0:T(1,128)S(1)} async-done(((f32[8,1,512]{2,1,0:T(1,128)}), f32[8,1,512]{2,1,0:T(1,128)S(1)}, u32[]{:S(2)}, u32[]{:S(2)}) %all-to-all-start) | async-done | bytes 16416 | tf_op jit(solution)/shard_map/all_to_all | solution.py:531
  15.2 0.0 copy-done.1
  15.2 0.0 copy-done.2
  15.2 0.0 copy-done.4
  15.2 6.8 %first_part.1 = (bf16[8,16,512]{2,1,0:T(8,128)(2,1)S(1)}, bf16[1328,512]{1,0:T(8,128)(2,1)S(1)}) custom-call(s32[1]{0:T(128)} %bitcast.place_ref, f32[8,1,512]{2,1,0:T(1,128)S(1)} %all-to-all-done.squares_ref, s32[1,512]{1,0:T(1,128)S(1)} %bitcast.6, s32[1,512]{1,0:T(1,128)S(1)} %bitcast.4, bf16[512,512]{1,0:T(8,128)(2,1)S(1)} %copy-done.1, ...), custom_call_target="tpu_custom_call" | custom-call | flops 1000000000 | bytes 4000000 | tf_op jit(solution)/shard_map/first_part/pallas_call | solution.py:536
  22.0 14.6 %all_to_all.15.rows_ref = bf16[8,16,512]{2,1,0:T(8,128)(2,1)S(1)} all-to-all(bf16[8,16,512]{2,1,0:T(8,128)(2,1)S(1)} %get-tuple-element.12), channel_id=1, replica_groups={{0,8,16,24,32,40,48,56},{64,72,80,88,96,104,112,120},{128,136,144,152,1..., dimensions={0} | all-to-all | bytes 262144 | tf_op jit(solution)/shard_map/all_to_all | solution.py:563
  36.6 0.0 copy-start.6
  36.6 0.7 %near_part.1 = (f32[16,512]{1,0:T(8,128)S(1)}, bf16[8,16,512]{2,1,0:T(8,128)(2,1)}) custom-call(s32[1]{0:T(128)} %bitcast.place_ref, bf16[8,16,512]{2,1,0:T(8,128)(2,1)S(1)} %all_to_all.15.rows_ref, f32[16,512]{1,0:T(8,128)S(1)} %copy-done.2), custom_call_target="tpu_custom_call" | custom-call | flops 1000000000 | bytes 4000000 | tf_op jit(solution)/shard_map/near_part/pallas_call | solution.py:574
  37.3 10.3 %all-to-all-start.2 = ((bf16[8,16,512]{2,1,0:T(8,128)(2,1)}), bf16[8,16,512]{2,1,0:T(8,128)(2,1)S(1)}, u32[]{:S(2)}, u32[]{:S(2)}) async-start(bf16[8,16,512]{2,1,0:T(8,128)(2,1)} %get-tuple-element.14), calls=%async_computation.2 | async-start | bytes 262144 | tf_op jit(solution)/shard_map/all_to_all | solution.py:581
  47.6 0.0 copy-done.6
  47.6 4.2 %second_part.1 = (bf16[512,512]{1,0:T(8,128)(2,1)S(1)}, f32[512,512]{1,0:T(8,128)S(1)}, f32[16,512]{1,0:T(8,128)S(1)}) custom-call(f32[2,3,7,512]{3,2,1,0:T(8,128)S(1)} %copy.12.filters_ref, f32[16,512]{1,0:T(8,128)S(1)} %copy-done.2, f32[16,512]{1,0:T(8,128)S(1)} %copy-done.6, bf16[1328,512]{1,0:T(8,128)(2,1)S(1)} %get-tuple-element.15.kept_ref, ...), custom_call_target="tpu_custom_call" | custom-call | flops 4000000000 | bytes 10000000 | tf_op jit(solution)/shard_map/second_part/pallas_call | solution.py:564
  51.8 4.9 %all-to-all-done.2.totals_ref = bf16[8,16,512]{2,1,0:T(8,128)(2,1)S(1)} async-done(((bf16[8,16,512]{2,1,0:T(8,128)(2,1)}), bf16[8,16,512]{2,1,0:T(8,128)(2,1)S(1)}, u32[]{:S(2)}, u32[]{:S(2)}) %all-to-all-start.2) | async-done | bytes 131104 | tf_op jit(solution)/shard_map/all_to_all | solution.py:581
  56.7 2.1 %third_part.1 = bf16[512,512]{1,0:T(8,128)(2,1)} custom-call(s32[1]{0:T(128)} %bitcast.place_ref, f32[16,512]{1,0:T(8,128)S(1)} %get-tuple-element.13.near_ref, bf16[8,16,512]{2,1,0:T(8,128)(2,1)S(1)} %all-to-all-done.2.totals_ref, f32[16,512]{1,0:T(8,128)S(1)} %copy-done.2, f32[16,512]{1,0:T(8,128)S(1)} %get-tuple-element.16.weights_ref, ...), custom_call_target="tpu_custom_call" | custom-call | flops 1000000000 | bytes 4000000 | tf_op jit(solution)/shard_map/third_part/pallas_call | solution.py:582
  (1 shorter events, 0.0 us)
Async XLA Ops:
  0.0 1.0 %copy-start = (bf16[512,512]{1,0:T(8,128)(2,1)S(1)}, bf16[512,512]{1,0:T(8,128)(2,1)}, u32[]{:S(2)}) copy-start(bf16[512,512]{1,0:T(8,128)(2,1)} %table_ref.3) | copy-start | bytes 1572868
  1.0 10.2 %copy-start.3 = (s32[512]{0:T(512)S(1)}, s32[512]{0:T(512)}, u32[]{:S(2)}) copy-start(s32[512]{0:T(512)} %param.11) | copy-start | bytes 6148
  1.0 11.7 %copy-start.5 = (f32[128,512]{1,0:T(8,128)S(1)}, f32[128,512]{1,0:T(8,128)}, u32[]{:S(2)}) copy-start(f32[128,512]{1,0:T(8,128)} %medium_ref.1) | copy-start | bytes 786436
  1.0 11.7 %copy-start.7 = (bf16[672,384]{1,0:T(8,128)(2,1)S(1)}, bf16[672,384]{1,0:T(8,128)(2,1)}, u32[]{:S(2)}) copy-start(bf16[672,384]{1,0:T(8,128)(2,1)} %constant.14.clone.wave_ref) | copy-start | bytes 1548292
  2.1 13.1 %all-to-all-start = ((f32[8,1,512]{2,1,0:T(1,128)}), f32[8,1,512]{2,1,0:T(1,128)S(1)}, u32[]{:S(2)}, u32[]{:S(2)}) async-start(f32[8,1,512]{2,1,0:T(1,128)} %square_sums.1), calls=%async_computation | async-start | bytes 32768 | tf_op jit(solution)/shard_map/all_to_all | solution.py:531
  11.2 2.0 %copy-start.8 = (f32[2,3,7,512]{3,0,2,1:T(2,128)S(1)}, f32[2,3,7,512]{3,0,2,1:T(2,128)}, u32[]{:S(2)}) copy-start(f32[2,3,7,512]{3,0,2,1:T(2,128)} %param.14) | copy-start | bytes 258052
  11.2 3.9 %copy-start.1 = (bf16[512,512]{1,0:T(8,128)(2,1)S(1)}, bf16[512,512]{1,0:T(8,128)(2,1)}, u32[]{:S(2)}) copy-start(bf16[512,512]{1,0:T(8,128)(2,1)} %table_ref.3) | copy-start | bytes 1572868
  11.3 3.9 %copy-start.2 = (f32[16,512]{1,0:T(8,128)S(1)}, f32[16,512]{1,0:T(8,128)}, u32[]{:S(2)}) copy-start(f32[16,512]{1,0:T(8,128)} %rates_ref.7) | copy-start | bytes 98308
  11.3 3.9 %copy-start.4 = (f32[512]{0:T(512)S(1)}, f32[512]{0:T(512)}, u32[]{:S(2)}) copy-start(f32[512]{0:T(512)} %param.13) | copy-start | bytes 6148
  11.3 2.7 %collective-permute-start = (s32[512]{0:T(512)S(1)}, s32[512]{0:T(512)S(1)}, u32[]{:S(2)}, u32[]{:S(2)}) collective-permute-start(s32[512]{0:T(512)S(1)} %copy-done.3), channel_id=1, source_target_pairs={{0,8},{8,16},{16,24},{24,32},{32,40},{40,48},{48,56},{56,64},{64,7... | collective-permute-start | bytes 6152 | tf_op jit(solution)/shard_map/ppermute | solution.py:527
  36.6 11.0 %copy-start.6 = (f32[16,512]{1,0:T(8,128)S(1)}, f32[16,512]{1,0:T(8,128)}, u32[]{:S(2)}) copy-start(f32[16,512]{1,0:T(8,128)} %residues_ref.1) | copy-start | bytes 98308
  37.3 19.4 %all-to-all-start.2 = ((bf16[8,16,512]{2,1,0:T(8,128)(2,1)}), bf16[8,16,512]{2,1,0:T(8,128)(2,1)S(1)}, u32[]{:S(2)}, u32[]{:S(2)}) async-start(bf16[8,16,512]{2,1,0:T(8,128)(2,1)} %get-tuple-element.14), calls=%async_computation.2 | async-start | bytes 262144 | tf_op jit(solution)/shard_map/all_to_all | solution.py:581

commit v2 on v1

--- a/solution.py
+++ b/solution.py
@@ -437,8 +437,9 @@
     own = lax.rem(place_ref[0], inner)
     rank = lax.div(place_ref[0], inner)
     far = jnp.zeros(rates_ref.shape, F32)
-    for j in range(totals_ref.shape[0]):
-        far = jnp.where(j < rank, across * far + totals_ref[j].astype(F32), far)
+    last = totals_ref.shape[0] - 1
+    for j in range(last + 1):
+        far = jnp.where(j < rank, across * far + totals_ref[last - j].astype(F32), far)
     incoming = near_ref[...] + jnp.exp(-rates_ref[...] * (span * own.astype(F32))) * far
 
     stores = []
@@ -520,7 +521,7 @@
     length = lax.axis_size("seq")
     inner = min(INNER, length)
     near_groups = [[o * inner + i for i in range(inner)] for o in range(length // inner)]
-    far_groups = [[o * inner + i for o in range(length // inner)] for i in range(inner)]
+    far_groups = [[o * inner + i for o in reversed(range(length // inner))] for i in range(inner)]
     const = tables(taps)
     place = jnp.reshape(lax.axis_index("seq").astype(jnp.int32), (1,))
 

time: 59.1 us -> 57.9 us (0.980)
  waiting for transfers between devices: 6.73 us -> 3.47 us
  starting transfers between devices: 20.9 us -> 22.9 us
    all_to_all x1, waiting for transfers between devices: 4.86 us -> 1.6 us  [local(): lax.all_to_all(totals, 'seq', 0, 0, axis_index_groups=far_groups, tiled=T...]
    all_to_all x1, starting transfers between devices: 10.3 us -> 12.4 us  [local(): lax.all_to_all(totals, 'seq', 0, 0, axis_index_groups=far_groups, tiled=T...]
where the time goes in v2:
time: 57.9 us; the launch traced here: 57.6 us
  starting transfers between devices  22.9 us (40%)
  Pallas kernels  15.4 us (27%)
  blocking collectives  14.6 us (25%)
  waiting for transfers between devices  3.47 us (6%)
  local copies, waits for them, and re-layouts  1.1 us (2%)
    all_to_all x1, blocking collectives, local(): lax.all_to_all(state, 'seq', 0, 0, axis_index_groups=near_groups, tiled=T...  14.6 us
    all_to_all x1, starting transfers between devices, local(): lax.all_to_all(totals, 'seq', 0, 0, axis_index_groups=far_groups, tiled=T...  12.4 us
    all_to_all x1, starting transfers between devices, local(): squares = lax.all_to_all(partial, 'ch', 0, 0)  9.15 us
    pallas_call x1, Pallas kernels, local(): call(functools.partial(first_part, channels_of(width, shards)), 'first_pa...  6.81 us
    pallas_call x1, Pallas kernels, local(): call(second_part, 'second_part', [VMEM] * 4 + [FAR], [((count, width), BF...  4.2 us
    pallas_call x1, Pallas kernels, local(): call(functools.partial(third_part, inner), 'third_part', [SMEM] + [VMEM]...  2.12 us
    all_to_all x1, waiting for transfers between devices, local(): lax.all_to_all(totals, 'seq', 0, 0, axis_index_groups=far_groups, tiled=T...  1.6 us
    ppermute x1, starting transfers between devices, local(): lax.ppermute(token_ids, 'seq', [(i, i + 1) for i in range(length - 1)])  1.42 us
  transfers between devices with their start and end apart: 3, of which 3 were waited for; matrix products, arithmetic and copies ran while one was open for 0% of the time, Pallas kernels for 8%

profile of v2, /device:TPU:2, one launch (start us, length us, event | category | flops | bytes accessed | tf_op | source)
XLA Modules:
  0.0 57.6 jit_solution(5935996925707041251)
XLA Ops:
  0.0 0.0 copy-start
  0.0 1.0 %copy-done = bf16[512,512]{1,0:T(8,128)(2,1)S(1)} copy-done((bf16[512,512]{1,0:T(8,128)(2,1)S(1)}, bf16[512,512]{1,0:T(8,128)(2,1)}, u32[]{:S(2)}) %copy-start) | copy-done | bytes 524312
  1.0 0.0 copy-start.3
  1.0 0.0 copy-start.5
  1.0 0.0 copy-start.7
  1.0 1.0 %square_sums.1 = f32[8,1,512]{2,1,0:T(1,128)} custom-call(bf16[512,512]{1,0:T(8,128)(2,1)S(1)} %copy-done), custom_call_target="tpu_custom_call" | custom-call | flops 1000000000 | bytes 4000000 | tf_op jit(solution)/shard_map/square_sums/pallas_call | solution.py:529
  2.1 9.2 %all-to-all-start = ((f32[8,1,512]{2,1,0:T(1,128)}), f32[8,1,512]{2,1,0:T(1,128)S(1)}, u32[]{:S(2)}, u32[]{:S(2)}) async-start(f32[8,1,512]{2,1,0:T(1,128)} %square_sums.1), calls=%async_computation | async-start | bytes 32768 | tf_op jit(solution)/shard_map/all_to_all | solution.py:532
  11.2 0.0 copy-done.3
  11.2 0.0 copy-start.8
  11.2 0.0 copy-start.1
  11.3 0.0 copy-start.2
  11.3 0.0 copy-start.4
  11.3 1.4 %collective-permute-start = (s32[512]{0:T(512)S(1)}, s32[512]{0:T(512)S(1)}, u32[]{:S(2)}, u32[]{:S(2)}) collective-permute-start(s32[512]{0:T(512)S(1)} %copy-done.3), channel_id=1, source_target_pairs={{0,8},{8,16},{16,24},{24,32},{32,40},{40,48},{48,56},{56,64},{64,7... | collective-permute-start | bytes 6152 | tf_op jit(solution)/shard_map/ppermute | solution.py:528
  12.7 0.0 copy-done.5
  12.7 0.0 copy-done.7
  12.7 0.5 spectrum_of.1.spectrum_ref
  13.3 0.0 copy-done.8
  13.3 0.7 %collective-permute-done = s32[512]{0:T(512)S(1)} collective-permute-done((s32[512]{0:T(512)S(1)}, s32[512]{0:T(512)S(1)}, u32[]{:S(2)}, u32[]{:S(2)}) %collective-permute-start) | collective-permute-done | bytes 2080 | tf_op jit(solution)/shard_map/ppermute | solution.py:528
  14.0 1.2 %all-to-all-done.squares_ref = f32[8,1,512]{2,1,0:T(1,128)S(1)} async-done(((f32[8,1,512]{2,1,0:T(1,128)}), f32[8,1,512]{2,1,0:T(1,128)S(1)}, u32[]{:S(2)}, u32[]{:S(2)}) %all-to-all-start) | async-done | bytes 16416 | tf_op jit(solution)/shard_map/all_to_all | solution.py:532
  15.2 0.0 copy-done.1
  15.2 0.0 copy-done.2
  15.2 0.0 copy-done.4
  15.2 6.8 %first_part.1 = (bf16[8,16,512]{2,1,0:T(8,128)(2,1)S(1)}, bf16[1328,512]{1,0:T(8,128)(2,1)S(1)}) custom-call(s32[1]{0:T(128)} %bitcast.place_ref, f32[8,1,512]{2,1,0:T(1,128)S(1)} %all-to-all-done.squares_ref, s32[1,512]{1,0:T(1,128)S(1)} %bitcast.6, s32[1,512]{1,0:T(1,128)S(1)} %bitcast.4, bf16[512,512]{1,0:T(8,128)(2,1)S(1)} %copy-done.1, ...), custom_call_target="tpu_custom_call" | custom-call | flops 1000000000 | bytes 4000000 | tf_op jit(solution)/shard_map/first_part/pallas_call | solution.py:537
  22.0 14.6 %all_to_all.15.rows_ref = bf16[8,16,512]{2,1,0:T(8,128)(2,1)S(1)} all-to-all(bf16[8,16,512]{2,1,0:T(8,128)(2,1)S(1)} %get-tuple-element.12), channel_id=1, replica_groups={{0,8,16,24,32,40,48,56},{64,72,80,88,96,104,112,120},{128,136,144,152,1..., dimensions={0} | all-to-all | bytes 262144 | tf_op jit(solution)/shard_map/all_to_all | solution.py:564
  36.6 0.0 copy-start.6
  36.6 0.7 %near_part.1 = (f32[16,512]{1,0:T(8,128)S(1)}, bf16[8,16,512]{2,1,0:T(8,128)(2,1)}) custom-call(s32[1]{0:T(128)} %bitcast.place_ref, bf16[8,16,512]{2,1,0:T(8,128)(2,1)S(1)} %all_to_all.15.rows_ref, f32[16,512]{1,0:T(8,128)S(1)} %copy-done.2), custom_call_target="tpu_custom_call" | custom-call | flops 1000000000 | bytes 4000000 | tf_op jit(solution)/shard_map/near_part/pallas_call | solution.py:575
  37.3 12.4 %all-to-all-start.2 = ((bf16[8,16,512]{2,1,0:T(8,128)(2,1)}), bf16[8,16,512]{2,1,0:T(8,128)(2,1)S(1)}, u32[]{:S(2)}, u32[]{:S(2)}) async-start(bf16[8,16,512]{2,1,0:T(8,128)(2,1)} %get-tuple-element.14), calls=%async_computation.2 | async-start | bytes 262144 | tf_op jit(solution)/shard_map/all_to_all | solution.py:582
  49.6 0.0 copy-done.6
  49.6 4.2 %second_part.1 = (bf16[512,512]{1,0:T(8,128)(2,1)S(1)}, f32[512,512]{1,0:T(8,128)S(1)}, f32[16,512]{1,0:T(8,128)S(1)}) custom-call(f32[2,3,7,512]{3,2,1,0:T(8,128)S(1)} %copy.12.filters_ref, f32[16,512]{1,0:T(8,128)S(1)} %copy-done.2, f32[16,512]{1,0:T(8,128)S(1)} %copy-done.6, bf16[1328,512]{1,0:T(8,128)(2,1)S(1)} %get-tuple-element.15.kept_ref, ...), custom_call_target="tpu_custom_call" | custom-call | flops 4000000000 | bytes 10000000 | tf_op jit(solution)/shard_map/second_part/pallas_call | solution.py:565
  53.9 1.6 %all-to-all-done.2.totals_ref = bf16[8,16,512]{2,1,0:T(8,128)(2,1)S(1)} async-done(((bf16[8,16,512]{2,1,0:T(8,128)(2,1)}), bf16[8,16,512]{2,1,0:T(8,128)(2,1)S(1)}, u32[]{:S(2)}, u32[]{:S(2)}) %all-to-all-start.2) | async-done | bytes 131104 | tf_op jit(solution)/shard_map/all_to_all | solution.py:582
  55.5 2.1 %third_part.1 = bf16[512,512]{1,0:T(8,128)(2,1)} custom-call(s32[1]{0:T(128)} %bitcast.place_ref, f32[16,512]{1,0:T(8,128)S(1)} %get-tuple-element.13.near_ref, bf16[8,16,512]{2,1,0:T(8,128)(2,1)S(1)} %all-to-all-done.2.totals_ref, f32[16,512]{1,0:T(8,128)S(1)} %copy-done.2, f32[16,512]{1,0:T(8,128)S(1)} %get-tuple-element.16.weights_ref, ...), custom_call_target="tpu_custom_call" | custom-call | flops 1000000000 | bytes 4000000 | tf_op jit(solution)/shard_map/third_part/pallas_call | solution.py:583
  (1 shorter events, 0.0 us)
Async XLA Ops:
  0.0 1.0 %copy-start = (bf16[512,512]{1,0:T(8,128)(2,1)S(1)}, bf16[512,512]{1,0:T(8,128)(2,1)}, u32[]{:S(2)}) copy-start(bf16[512,512]{1,0:T(8,128)(2,1)} %table_ref.3) | copy-start | bytes 1572868
  1.0 10.2 %copy-start.3 = (s32[512]{0:T(512)S(1)}, s32[512]{0:T(512)}, u32[]{:S(2)}) copy-start(s32[512]{0:T(512)} %param.11) | copy-start | bytes 6148
  1.0 11.7 %copy-start.5 = (f32[128,512]{1,0:T(8,128)S(1)}, f32[128,512]{1,0:T(8,128)}, u32[]{:S(2)}) copy-start(f32[128,512]{1,0:T(8,128)} %medium_ref.1) | copy-start | bytes 786436
  1.0 11.7 %copy-start.7 = (bf16[672,384]{1,0:T(8,128)(2,1)S(1)}, bf16[672,384]{1,0:T(8,128)(2,1)}, u32[]{:S(2)}) copy-start(bf16[672,384]{1,0:T(8,128)(2,1)} %constant.14.clone.wave_ref) | copy-start | bytes 1548292
  2.1 13.1 %all-to-all-start = ((f32[8,1,512]{2,1,0:T(1,128)}), f32[8,1,512]{2,1,0:T(1,128)S(1)}, u32[]{:S(2)}, u32[]{:S(2)}) async-start(f32[8,1,512]{2,1,0:T(1,128)} %square_sums.1), calls=%async_computation | async-start | bytes 32768 | tf_op jit(solution)/shard_map/all_to_all | solution.py:532
  11.2 2.0 %copy-start.8 = (f32[2,3,7,512]{3,0,2,1:T(2,128)S(1)}, f32[2,3,7,512]{3,0,2,1:T(2,128)}, u32[]{:S(2)}) copy-start(f32[2,3,7,512]{3,0,2,1:T(2,128)} %param.14) | copy-start | bytes 258052
  11.2 3.9 %copy-start.1 = (bf16[512,512]{1,0:T(8,128)(2,1)S(1)}, bf16[512,512]{1,0:T(8,128)(2,1)}, u32[]{:S(2)}) copy-start(bf16[512,512]{1,0:T(8,128)(2,1)} %table_ref.3) | copy-start | bytes 1572868
  11.3 3.9 %copy-start.2 = (f32[16,512]{1,0:T(8,128)S(1)}, f32[16,512]{1,0:T(8,128)}, u32[]{:S(2)}) copy-start(f32[16,512]{1,0:T(8,128)} %rates_ref.7) | copy-start | bytes 98308
  11.3 3.9 %copy-start.4 = (f32[512]{0:T(512)S(1)}, f32[512]{0:T(512)}, u32[]{:S(2)}) copy-start(f32[512]{0:T(512)} %param.13) | copy-start | bytes 6148
  11.3 2.7 %collective-permute-start = (s32[512]{0:T(512)S(1)}, s32[512]{0:T(512)S(1)}, u32[]{:S(2)}, u32[]{:S(2)}) collective-permute-start(s32[512]{0:T(512)S(1)} %copy-done.3), channel_id=1, source_target_pairs={{0,8},{8,16},{16,24},{24,32},{32,40},{40,48},{48,56},{56,64},{64,7... | collective-permute-start | bytes 6152 | tf_op jit(solution)/shard_map/ppermute | solution.py:528
  36.6 13.1 %copy-start.6 = (f32[16,512]{1,0:T(8,128)S(1)}, f32[16,512]{1,0:T(8,128)}, u32[]{:S(2)}) copy-start(f32[16,512]{1,0:T(8,128)} %residues_ref.1) | copy-start | bytes 98308
  37.3 18.2 %all-to-all-start.2 = ((bf16[8,16,512]{2,1,0:T(8,128)(2,1)}), bf16[8,16,512]{2,1,0:T(8,128)(2,1)S(1)}, u32[]{:S(2)}, u32[]{:S(2)}) async-start(bf16[8,16,512]{2,1,0:T(8,128)(2,1)} %get-tuple-element.14), calls=%async_computation.2 | async-start | bytes 262144 | tf_op jit(solution)/shard_map/all_to_all | solution.py:582

commit v3 on v2

--- a/solution.py
+++ b/solution.py
@@ -21,7 +21,7 @@
 HALO_IDS = 256
 BLOCK = 16
 SECOND_ROWS = (SPAN + STEPS) * LINES
-FREQS = 672
+FREQS = 656
 INNER = 8
 NT = (((1,), (1,)), ((), ()))
 
@@ -333,14 +333,24 @@
     return residues * jnp.sqrt(jnp.where(double < 0.02, series, 1.0 - jnp.exp(-double)))
 
 
+def near_order(inner):
+    late = inner // 2
+    order = [late]
+    for step in range(late):
+        order += [place for place in (step, inner - step) if place % inner not in order and place < inner]
+    order += [place for place in range(inner) if place not in order]
+    return order[:0:-1] + order[:1]
+
+
 def near_part(place_ref, rows_ref, rates_ref, near_ref, total_ref):
     across = jnp.exp(-rates_ref[...] * (1.0 * STEPS * LINES))
     own = lax.rem(place_ref[0], rows_ref.shape[0])
     total = jnp.zeros(rates_ref.shape, F32)
     near = total
+    order = near_order(rows_ref.shape[0])
     for j in range(rows_ref.shape[0]):
         near = jnp.where(own == j, total, near)
-        total = across * total + rows_ref[j].astype(F32)
+        total = across * total + rows_ref[order.index(j)].astype(F32)
     near_ref[...] = near
     total_ref[...] = jnp.broadcast_to(total.astype(BF16)[None], total_ref.shape)
 
@@ -520,7 +530,7 @@
     shards = lax.axis_size("ch")
     length = lax.axis_size("seq")
     inner = min(INNER, length)
-    near_groups = [[o * inner + i for i in range(inner)] for o in range(length // inner)]
+    near_groups = [[o * inner + i for i in near_order(inner)] for o in range(length // inner)]
     far_groups = [[o * inner + i for o in reversed(range(length // inner))] for i in range(inner)]
     const = tables(taps)
     place = jnp.reshape(lax.axis_index("seq").astype(jnp.int32), (1,))

time: 57.9 us -> 54 us (0.933)
  blocking collectives: 14.6 us -> 11.3 us
  starting transfers between devices: 22.9 us -> 22.2 us
    all_to_all x1, blocking collectives: 14.6 us -> 11.3 us  [local(): lax.all_to_all(state, 'seq', 0, 0, axis_index_groups=near_groups, tiled=T...]
    all_to_all x1, starting transfers between devices: 12.4 us -> 11.7 us  [local(): lax.all_to_all(totals, 'seq', 0, 0, axis_index_groups=far_groups, tiled=T...]
  transfers between devices with their start and end apart: 3 -> 3, of which waited for: 3 -> 3; matrix products, arithmetic and copies ran while one was open for 0% -> 0% of each run, Pallas kernels for 8% -> 9%
where the time goes in v3:
time: 54 us; the launch traced here: 53.7 us
  starting transfers between devices  22.2 us (41%)
  Pallas kernels  15.4 us (29%)
  blocking collectives  11.3 us (21%)
  waiting for transfers between devices  3.59 us (7%)
  local copies, waits for them, and re-layouts  1.1 us (2%)
    all_to_all x1, starting transfers between devices, local(): lax.all_to_all(totals, 'seq', 0, 0, axis_index_groups=far_groups, tiled=T...  11.7 us
    all_to_all x1, blocking collectives, local(): lax.all_to_all(state, 'seq', 0, 0, axis_index_groups=near_groups, tiled=T...  11.3 us
    all_to_all x1, starting transfers between devices, local(): squares = lax.all_to_all(partial, 'ch', 0, 0)  9.15 us
    pallas_call x1, Pallas kernels, local(): call(functools.partial(first_part, channels_of(width, shards)), 'first_pa...  6.79 us
    pallas_call x1, Pallas kernels, local(): call(second_part, 'second_part', [VMEM] * 4 + [FAR], [((count, width), BF...  4.2 us
    pallas_call x1, Pallas kernels, local(): call(functools.partial(third_part, inner), 'third_part', [SMEM] + [VMEM]...  2.12 us
    all_to_all x1, waiting for transfers between devices, local(): lax.all_to_all(totals, 'seq', 0, 0, axis_index_groups=far_groups, tiled=T...  1.71 us
    ppermute x1, starting transfers between devices, local(): lax.ppermute(token_ids, 'seq', [(i, i + 1) for i in range(length - 1)])  1.42 us
  transfers between devices with their start and end apart: 3, of which 3 were waited for; matrix products, arithmetic and copies ran while one was open for 0% of the time, Pallas kernels for 9%

profile of v3, /device:TPU:2, one launch (start us, length us, event | category | flops | bytes accessed | tf_op | source)
XLA Modules:
  0.0 53.7 jit_solution(8370782362737440467)
XLA Ops:
  0.0 0.0 copy-start
  0.0 1.0 %copy-done = bf16[512,512]{1,0:T(8,128)(2,1)S(1)} copy-done((bf16[512,512]{1,0:T(8,128)(2,1)S(1)}, bf16[512,512]{1,0:T(8,128)(2,1)}, u32[]{:S(2)}) %copy-start) | copy-done | bytes 524312
  1.0 0.0 copy-start.3
  1.0 0.0 copy-start.5
  1.0 0.0 copy-start.7
  1.0 1.0 %square_sums.1 = f32[8,1,512]{2,1,0:T(1,128)} custom-call(bf16[512,512]{1,0:T(8,128)(2,1)S(1)} %copy-done), custom_call_target="tpu_custom_call" | custom-call | flops 1000000000 | bytes 4000000 | tf_op jit(solution)/shard_map/square_sums/pallas_call | solution.py:539
  2.1 9.2 %all-to-all-start = ((f32[8,1,512]{2,1,0:T(1,128)}), f32[8,1,512]{2,1,0:T(1,128)S(1)}, u32[]{:S(2)}, u32[]{:S(2)}) async-start(f32[8,1,512]{2,1,0:T(1,128)} %square_sums.1), calls=%async_computation | async-start | bytes 32768 | tf_op jit(solution)/shard_map/all_to_all | solution.py:542
  11.2 0.0 copy-done.3
  11.2 0.0 copy-start.8
  11.2 0.0 copy-start.1
  11.3 0.0 copy-start.2
  11.3 0.0 copy-start.4
  11.3 1.4 %collective-permute-start = (s32[512]{0:T(512)S(1)}, s32[512]{0:T(512)S(1)}, u32[]{:S(2)}, u32[]{:S(2)}) collective-permute-start(s32[512]{0:T(512)S(1)} %copy-done.3), channel_id=1, source_target_pairs={{0,8},{8,16},{16,24},{24,32},{32,40},{40,48},{48,56},{56,64},{64,7... | collective-permute-start | bytes 6152 | tf_op jit(solution)/shard_map/ppermute | solution.py:538
  12.7 0.0 copy-done.5
  12.7 0.0 copy-done.7
  12.7 0.5 spectrum_of.1.spectrum_ref
  13.2 0.0 copy-done.8
  13.3 0.7 %collective-permute-done = s32[512]{0:T(512)S(1)} collective-permute-done((s32[512]{0:T(512)S(1)}, s32[512]{0:T(512)S(1)}, u32[]{:S(2)}, u32[]{:S(2)}) %collective-permute-start) | collective-permute-done | bytes 2080 | tf_op jit(solution)/shard_map/ppermute | solution.py:538
  14.0 1.2 %all-to-all-done.squares_ref = f32[8,1,512]{2,1,0:T(1,128)S(1)} async-done(((f32[8,1,512]{2,1,0:T(1,128)}), f32[8,1,512]{2,1,0:T(1,128)S(1)}, u32[]{:S(2)}, u32[]{:S(2)}) %all-to-all-start) | async-done | bytes 16416 | tf_op jit(solution)/shard_map/all_to_all | solution.py:542
  15.2 0.0 copy-done.1
  15.2 0.0 copy-done.2
  15.2 0.0 copy-done.4
  15.2 6.8 %first_part.1 = (bf16[8,16,512]{2,1,0:T(8,128)(2,1)S(1)}, bf16[1328,512]{1,0:T(8,128)(2,1)S(1)}) custom-call(s32[1]{0:T(128)} %bitcast.place_ref, f32[8,1,512]{2,1,0:T(1,128)S(1)} %all-to-all-done.squares_ref, s32[1,512]{1,0:T(1,128)S(1)} %bitcast.6, s32[1,512]{1,0:T(1,128)S(1)} %bitcast.4, bf16[512,512]{1,0:T(8,128)(2,1)S(1)} %copy-done.1, ...), custom_call_target="tpu_custom_call" | custom-call | flops 1000000000 | bytes 4000000 | tf_op jit(solution)/shard_map/first_part/pallas_call | solution.py:547
  22.0 11.3 %all_to_all.15.rows_ref = bf16[8,16,512]{2,1,0:T(8,128)(2,1)S(1)} all-to-all(bf16[8,16,512]{2,1,0:T(8,128)(2,1)S(1)} %get-tuple-element.12), channel_id=1, replica_groups={{40,24,48,16,56,8,0,32},{104,88,112,80,120,72,64,96},{168,152,176,144,1..., dimensions={0} | all-to-all | bytes 262144 | tf_op jit(solution)/shard_map/all_to_all | solution.py:574
  33.2 0.0 copy-start.6
  33.2 0.7 %near_part.1 = (f32[16,512]{1,0:T(8,128)S(1)}, bf16[8,16,512]{2,1,0:T(8,128)(2,1)}) custom-call(s32[1]{0:T(128)} %bitcast.place_ref, bf16[8,16,512]{2,1,0:T(8,128)(2,1)S(1)} %all_to_all.15.rows_ref, f32[16,512]{1,0:T(8,128)S(1)} %copy-done.2), custom_call_target="tpu_custom_call" | custom-call | flops 1000000000 | bytes 4000000 | tf_op jit(solution)/shard_map/near_part/pallas_call | solution.py:585
  33.9 11.7 %all-to-all-start.2 = ((bf16[8,16,512]{2,1,0:T(8,128)(2,1)}), bf16[8,16,512]{2,1,0:T(8,128)(2,1)S(1)}, u32[]{:S(2)}, u32[]{:S(2)}) async-start(bf16[8,16,512]{2,1,0:T(8,128)(2,1)} %get-tuple-element.14), calls=%async_computation.2 | async-start | bytes 262144 | tf_op jit(solution)/shard_map/all_to_all | solution.py:592
  45.6 0.0 copy-done.6
  45.6 4.2 %second_part.1 = (bf16[512,512]{1,0:T(8,128)(2,1)S(1)}, f32[512,512]{1,0:T(8,128)S(1)}, f32[16,512]{1,0:T(8,128)S(1)}) custom-call(f32[2,3,7,512]{3,2,1,0:T(8,128)S(1)} %copy.12.filters_ref, f32[16,512]{1,0:T(8,128)S(1)} %copy-done.2, f32[16,512]{1,0:T(8,128)S(1)} %copy-done.6, bf16[1328,512]{1,0:T(8,128)(2,1)S(1)} %get-tuple-element.15.kept_ref, ...), custom_call_target="tpu_custom_call" | custom-call | flops 4000000000 | bytes 10000000 | tf_op jit(solution)/shard_map/second_part/pallas_call | solution.py:575
  49.8 1.7 %all-to-all-done.2.totals_ref = bf16[8,16,512]{2,1,0:T(8,128)(2,1)S(1)} async-done(((bf16[8,16,512]{2,1,0:T(8,128)(2,1)}), bf16[8,16,512]{2,1,0:T(8,128)(2,1)S(1)}, u32[]{:S(2)}, u32[]{:S(2)}) %all-to-all-start.2) | async-done | bytes 131104 | tf_op jit(solution)/shard_map/all_to_all | solution.py:592
  51.5 2.1 %third_part.1 = bf16[512,512]{1,0:T(8,128)(2,1)} custom-call(s32[1]{0:T(128)} %bitcast.place_ref, f32[16,512]{1,0:T(8,128)S(1)} %get-tuple-element.13.near_ref, bf16[8,16,512]{2,1,0:T(8,128)(2,1)S(1)} %all-to-all-done.2.totals_ref, f32[16,512]{1,0:T(8,128)S(1)} %copy-done.2, f32[16,512]{1,0:T(8,128)S(1)} %get-tuple-element.16.weights_ref, ...), custom_call_target="tpu_custom_call" | custom-call | flops 1000000000 | bytes 4000000 | tf_op jit(solution)/shard_map/third_part/pallas_call | solution.py:593
  (1 shorter events, 0.0 us)
Async XLA Ops:
  0.0 1.0 %copy-start = (bf16[512,512]{1,0:T(8,128)(2,1)S(1)}, bf16[512,512]{1,0:T(8,128)(2,1)}, u32[]{:S(2)}) copy-start(bf16[512,512]{1,0:T(8,128)(2,1)} %table_ref.3) | copy-start | bytes 1572868
  1.0 10.2 %copy-start.3 = (s32[512]{0:T(512)S(1)}, s32[512]{0:T(512)}, u32[]{:S(2)}) copy-start(s32[512]{0:T(512)} %param.11) | copy-start | bytes 6148
  1.0 11.7 %copy-start.5 = (f32[128,512]{1,0:T(8,128)S(1)}, f32[128,512]{1,0:T(8,128)}, u32[]{:S(2)}) copy-start(f32[128,512]{1,0:T(8,128)} %medium_ref.1) | copy-start | bytes 786436
  1.0 11.7 %copy-start.7 = (bf16[656,384]{1,0:T(8,128)(2,1)S(1)}, bf16[656,384]{1,0:T(8,128)(2,1)}, u32[]{:S(2)}) copy-start(bf16[656,384]{1,0:T(8,128)(2,1)} %constant.14.clone.wave_ref) | copy-start | bytes 1511428
  2.1 13.1 %all-to-all-start = ((f32[8,1,512]{2,1,0:T(1,128)}), f32[8,1,512]{2,1,0:T(1,128)S(1)}, u32[]{:S(2)}, u32[]{:S(2)}) async-start(f32[8,1,512]{2,1,0:T(1,128)} %square_sums.1), calls=%async_computation | async-start | bytes 32768 | tf_op jit(solution)/shard_map/all_to_all | solution.py:542
  11.2 2.0 %copy-start.8 = (f32[2,3,7,512]{3,0,2,1:T(2,128)S(1)}, f32[2,3,7,512]{3,0,2,1:T(2,128)}, u32[]{:S(2)}) copy-start(f32[2,3,7,512]{3,0,2,1:T(2,128)} %param.14) | copy-start | bytes 258052
  11.2 3.9 %copy-start.1 = (bf16[512,512]{1,0:T(8,128)(2,1)S(1)}, bf16[512,512]{1,0:T(8,128)(2,1)}, u32[]{:S(2)}) copy-start(bf16[512,512]{1,0:T(8,128)(2,1)} %table_ref.3) | copy-start | bytes 1572868
  11.3 3.9 %copy-start.2 = (f32[16,512]{1,0:T(8,128)S(1)}, f32[16,512]{1,0:T(8,128)}, u32[]{:S(2)}) copy-start(f32[16,512]{1,0:T(8,128)} %rates_ref.7) | copy-start | bytes 98308
  11.3 3.9 %copy-start.4 = (f32[512]{0:T(512)S(1)}, f32[512]{0:T(512)}, u32[]{:S(2)}) copy-start(f32[512]{0:T(512)} %param.13) | copy-start | bytes 6148
  11.3 2.7 %collective-permute-start = (s32[512]{0:T(512)S(1)}, s32[512]{0:T(512)S(1)}, u32[]{:S(2)}, u32[]{:S(2)}) collective-permute-start(s32[512]{0:T(512)S(1)} %copy-done.3), channel_id=1, source_target_pairs={{0,8},{8,16},{16,24},{24,32},{32,40},{40,48},{48,56},{56,64},{64,7... | collective-permute-start | bytes 6152 | tf_op jit(solution)/shard_map/ppermute | solution.py:538
  33.2 12.4 %copy-start.6 = (f32[16,512]{1,0:T(8,128)S(1)}, f32[16,512]{1,0:T(8,128)}, u32[]{:S(2)}) copy-start(f32[16,512]{1,0:T(8,128)} %residues_ref.1) | copy-start | bytes 98308
  33.9 17.6 %all-to-all-start.2 = ((bf16[8,16,512]{2,1,0:T(8,128)(2,1)}), bf16[8,16,512]{2,1,0:T(8,128)(2,1)S(1)}, u32[]{:S(2)}, u32[]{:S(2)}) async-start(bf16[8,16,512]{2,1,0:T(8,128)(2,1)} %get-tuple-element.14), calls=%async_computation.2 | async-start | bytes 262144 | tf_op jit(solution)/shard_map/all_to_all | solution.py:592

commit v4 on v3

--- a/solution.py
+++ b/solution.py
@@ -342,6 +342,10 @@
     return order[:0:-1] + order[:1]
 
 
+def far_order(outer):
+    return list(range(outer - 2, -1, -1)) + [outer - 1]
+
+
 def near_part(place_ref, rows_ref, rates_ref, near_ref, total_ref):
     across = jnp.exp(-rates_ref[...] * (1.0 * STEPS * LINES))
     own = lax.rem(place_ref[0], rows_ref.shape[0])
@@ -447,9 +451,9 @@
     own = lax.rem(place_ref[0], inner)
     rank = lax.div(place_ref[0], inner)
     far = jnp.zeros(rates_ref.shape, F32)
-    last = totals_ref.shape[0] - 1
-    for j in range(last + 1):
-        far = jnp.where(j < rank, across * far + totals_ref[last - j].astype(F32), far)
+    order = far_order(totals_ref.shape[0])
+    for j in range(totals_ref.shape[0]):
+        far = jnp.where(j < rank, across * far + totals_ref[order.index(j)].astype(F32), far)
     incoming = near_ref[...] + jnp.exp(-rates_ref[...] * (span * own.astype(F32))) * far
 
     stores = []
@@ -531,7 +535,7 @@
     length = lax.axis_size("seq")
     inner = min(INNER, length)
     near_groups = [[o * inner + i for i in near_order(inner)] for o in range(length // inner)]
-    far_groups = [[o * inner + i for o in reversed(range(length // inner))] for i in range(inner)]
+    far_groups = [[o * inner + i for o in far_order(length // inner)] for i in range(inner)]
     const = tables(taps)
     place = jnp.reshape(lax.axis_index("seq").astype(jnp.int32), (1,))
 

time: 54 us -> 53.2 us (0.985)
  waiting for transfers between devices: 3.59 us -> 2.82 us
    all_to_all x1, waiting for transfers between devices: 1.71 us -> 0.94 us  [local(): lax.all_to_all(totals, 'seq', 0, 0, axis_index_groups=far_groups, tiled=T...]
where the time goes in v4:
time: 53.2 us; the launch traced here: 52.9 us
  starting transfers between devices  22.2 us (42%)
  Pallas kernels  15.4 us (29%)
  blocking collectives  11.3 us (21%)
  waiting for transfers between devices  2.82 us (5%)
  local copies, waits for them, and re-layouts  1.1 us (2%)
    all_to_all x1, starting transfers between devices, local(): lax.all_to_all(totals, 'seq', 0, 0, axis_index_groups=far_groups, tiled=T...  11.6 us
    all_to_all x1, blocking collectives, local(): lax.all_to_all(state, 'seq', 0, 0, axis_index_groups=near_groups, tiled=T...  11.3 us
    all_to_all x1, starting transfers between devices, local(): squares = lax.all_to_all(partial, 'ch', 0, 0)  9.15 us
    pallas_call x1, Pallas kernels, local(): call(functools.partial(first_part, channels_of(width, shards)), 'first_pa...  6.79 us
    pallas_call x1, Pallas kernels, local(): call(second_part, 'second_part', [VMEM] * 4 + [FAR], [((count, width), BF...  4.2 us
    pallas_call x1, Pallas kernels, local(): call(functools.partial(third_part, inner), 'third_part', [SMEM] + [VMEM]...  2.12 us
    ppermute x1, starting transfers between devices, local(): lax.ppermute(token_ids, 'seq', [(i, i + 1) for i in range(length - 1)])  1.42 us
    all_to_all x1, waiting for transfers between devices, local(): squares = lax.all_to_all(partial, 'ch', 0, 0)  1.17 us
  transfers between devices with their start and end apart: 3, of which 3 were waited for; matrix products, arithmetic and copies ran while one was open for 0% of the time, Pallas kernels for 9%

profile of v4, /device:TPU:2, one launch (start us, length us, event | category | flops | bytes accessed | tf_op | source)
XLA Modules:
  0.0 52.9 jit_solution(6134636593179065567)
XLA Ops:
  0.0 0.0 copy-start
  0.0 1.0 %copy-done = bf16[512,512]{1,0:T(8,128)(2,1)S(1)} copy-done((bf16[512,512]{1,0:T(8,128)(2,1)S(1)}, bf16[512,512]{1,0:T(8,128)(2,1)}, u32[]{:S(2)}) %copy-start) | copy-done | bytes 524312
  1.0 0.0 copy-start.3
  1.0 0.0 copy-start.5
  1.0 0.0 copy-start.7
  1.0 1.0 %square_sums.1 = f32[8,1,512]{2,1,0:T(1,128)} custom-call(bf16[512,512]{1,0:T(8,128)(2,1)S(1)} %copy-done), custom_call_target="tpu_custom_call" | custom-call | flops 1000000000 | bytes 4000000 | tf_op jit(solution)/shard_map/square_sums/pallas_call | solution.py:543
  2.1 9.2 %all-to-all-start = ((f32[8,1,512]{2,1,0:T(1,128)}), f32[8,1,512]{2,1,0:T(1,128)S(1)}, u32[]{:S(2)}, u32[]{:S(2)}) async-start(f32[8,1,512]{2,1,0:T(1,128)} %square_sums.1), calls=%async_computation | async-start | bytes 32768 | tf_op jit(solution)/shard_map/all_to_all | solution.py:546
  11.2 0.0 copy-done.3
  11.2 0.0 copy-start.8
  11.2 0.0 copy-start.1
  11.3 0.0 copy-start.2
  11.3 0.0 copy-start.4
  11.3 1.4 %collective-permute-start = (s32[512]{0:T(512)S(1)}, s32[512]{0:T(512)S(1)}, u32[]{:S(2)}, u32[]{:S(2)}) collective-permute-start(s32[512]{0:T(512)S(1)} %copy-done.3), channel_id=1, source_target_pairs={{0,8},{8,16},{16,24},{24,32},{32,40},{40,48},{48,56},{56,64},{64,7... | collective-permute-start | bytes 6152 | tf_op jit(solution)/shard_map/ppermute | solution.py:542
  12.7 0.0 copy-done.5
  12.7 0.0 copy-done.7
  12.7 0.5 spectrum_of.1.spectrum_ref
  13.2 0.0 copy-done.8
  13.3 0.7 %collective-permute-done = s32[512]{0:T(512)S(1)} collective-permute-done((s32[512]{0:T(512)S(1)}, s32[512]{0:T(512)S(1)}, u32[]{:S(2)}, u32[]{:S(2)}) %collective-permute-start) | collective-permute-done | bytes 2080 | tf_op jit(solution)/shard_map/ppermute | solution.py:542
  14.0 1.2 %all-to-all-done.squares_ref = f32[8,1,512]{2,1,0:T(1,128)S(1)} async-done(((f32[8,1,512]{2,1,0:T(1,128)}), f32[8,1,512]{2,1,0:T(1,128)S(1)}, u32[]{:S(2)}, u32[]{:S(2)}) %all-to-all-start) | async-done | bytes 16416 | tf_op jit(solution)/shard_map/all_to_all | solution.py:546
  15.2 0.0 copy-done.1
  15.2 0.0 copy-done.2
  15.2 0.0 copy-done.4
  15.2 6.8 %first_part.1 = (bf16[8,16,512]{2,1,0:T(8,128)(2,1)S(1)}, bf16[1328,512]{1,0:T(8,128)(2,1)S(1)}) custom-call(s32[1]{0:T(128)} %bitcast.place_ref, f32[8,1,512]{2,1,0:T(1,128)S(1)} %all-to-all-done.squares_ref, s32[1,512]{1,0:T(1,128)S(1)} %bitcast.6, s32[1,512]{1,0:T(1,128)S(1)} %bitcast.4, bf16[512,512]{1,0:T(8,128)(2,1)S(1)} %copy-done.1, ...), custom_call_target="tpu_custom_call" | custom-call | flops 1000000000 | bytes 4000000 | tf_op jit(solution)/shard_map/first_part/pallas_call | solution.py:551
  22.0 11.3 %all_to_all.15.rows_ref = bf16[8,16,512]{2,1,0:T(8,128)(2,1)S(1)} all-to-all(bf16[8,16,512]{2,1,0:T(8,128)(2,1)S(1)} %get-tuple-element.12), channel_id=1, replica_groups={{40,24,48,16,56,8,0,32},{104,88,112,80,120,72,64,96},{168,152,176,144,1..., dimensions={0} | all-to-all | bytes 262144 | tf_op jit(solution)/shard_map/all_to_all | solution.py:578
  33.2 0.0 copy-start.6
  33.2 0.7 %near_part.1 = (f32[16,512]{1,0:T(8,128)S(1)}, bf16[8,16,512]{2,1,0:T(8,128)(2,1)}) custom-call(s32[1]{0:T(128)} %bitcast.place_ref, bf16[8,16,512]{2,1,0:T(8,128)(2,1)S(1)} %all_to_all.15.rows_ref, f32[16,512]{1,0:T(8,128)S(1)} %copy-done.2), custom_call_target="tpu_custom_call" | custom-call | flops 1000000000 | bytes 4000000 | tf_op jit(solution)/shard_map/near_part/pallas_call | solution.py:589
  33.9 11.6 %all-to-all-start.2 = ((bf16[8,16,512]{2,1,0:T(8,128)(2,1)}), bf16[8,16,512]{2,1,0:T(8,128)(2,1)S(1)}, u32[]{:S(2)}, u32[]{:S(2)}) async-start(bf16[8,16,512]{2,1,0:T(8,128)(2,1)} %get-tuple-element.14), calls=%async_computation.2 | async-start | bytes 262144 | tf_op jit(solution)/shard_map/all_to_all | solution.py:596
  45.6 0.0 copy-done.6
  45.6 4.2 %second_part.1 = (bf16[512,512]{1,0:T(8,128)(2,1)S(1)}, f32[512,512]{1,0:T(8,128)S(1)}, f32[16,512]{1,0:T(8,128)S(1)}) custom-call(f32[2,3,7,512]{3,2,1,0:T(8,128)S(1)} %copy.12.filters_ref, f32[16,512]{1,0:T(8,128)S(1)} %copy-done.2, f32[16,512]{1,0:T(8,128)S(1)} %copy-done.6, bf16[1328,512]{1,0:T(8,128)(2,1)S(1)} %get-tuple-element.15.kept_ref, ...), custom_call_target="tpu_custom_call" | custom-call | flops 4000000000 | bytes 10000000 | tf_op jit(solution)/shard_map/second_part/pallas_call | solution.py:579
  49.8 0.9 %all-to-all-done.2.totals_ref = bf16[8,16,512]{2,1,0:T(8,128)(2,1)S(1)} async-done(((bf16[8,16,512]{2,1,0:T(8,128)(2,1)}), bf16[8,16,512]{2,1,0:T(8,128)(2,1)S(1)}, u32[]{:S(2)}, u32[]{:S(2)}) %all-to-all-start.2) | async-done | bytes 131104 | tf_op jit(solution)/shard_map/all_to_all | solution.py:596
  50.7 2.1 %third_part.1 = bf16[512,512]{1,0:T(8,128)(2,1)} custom-call(s32[1]{0:T(128)} %bitcast.place_ref, f32[16,512]{1,0:T(8,128)S(1)} %get-tuple-element.13.near_ref, bf16[8,16,512]{2,1,0:T(8,128)(2,1)S(1)} %all-to-all-done.2.totals_ref, f32[16,512]{1,0:T(8,128)S(1)} %copy-done.2, f32[16,512]{1,0:T(8,128)S(1)} %get-tuple-element.16.weights_ref, ...), custom_call_target="tpu_custom_call" | custom-call | flops 1000000000 | bytes 4000000 | tf_op jit(solution)/shard_map/third_part/pallas_call | solution.py:597
  (1 shorter events, 0.0 us)
Async XLA Ops:
  0.0 1.0 %copy-start = (bf16[512,512]{1,0:T(8,128)(2,1)S(1)}, bf16[512,512]{1,0:T(8,128)(2,1)}, u32[]{:S(2)}) copy-start(bf16[512,512]{1,0:T(8,128)(2,1)} %table_ref.3) | copy-start | bytes 1572868
  1.0 10.2 %copy-start.3 = (s32[512]{0:T(512)S(1)}, s32[512]{0:T(512)}, u32[]{:S(2)}) copy-start(s32[512]{0:T(512)} %param.11) | copy-start | bytes 6148
  1.0 11.7 %copy-start.5 = (f32[128,512]{1,0:T(8,128)S(1)}, f32[128,512]{1,0:T(8,128)}, u32[]{:S(2)}) copy-start(f32[128,512]{1,0:T(8,128)} %medium_ref.1) | copy-start | bytes 786436
  1.0 11.7 %copy-start.7 = (bf16[656,384]{1,0:T(8,128)(2,1)S(1)}, bf16[656,384]{1,0:T(8,128)(2,1)}, u32[]{:S(2)}) copy-start(bf16[656,384]{1,0:T(8,128)(2,1)} %constant.14.clone.wave_ref) | copy-start | bytes 1511428
  2.1 13.1 %all-to-all-start = ((f32[8,1,512]{2,1,0:T(1,128)}), f32[8,1,512]{2,1,0:T(1,128)S(1)}, u32[]{:S(2)}, u32[]{:S(2)}) async-start(f32[8,1,512]{2,1,0:T(1,128)} %square_sums.1), calls=%async_computation | async-start | bytes 32768 | tf_op jit(solution)/shard_map/all_to_all | solution.py:546
  11.2 2.0 %copy-start.8 = (f32[2,3,7,512]{3,0,2,1:T(2,128)S(1)}, f32[2,3,7,512]{3,0,2,1:T(2,128)}, u32[]{:S(2)}) copy-start(f32[2,3,7,512]{3,0,2,1:T(2,128)} %param.14) | copy-start | bytes 258052
  11.2 3.9 %copy-start.1 = (bf16[512,512]{1,0:T(8,128)(2,1)S(1)}, bf16[512,512]{1,0:T(8,128)(2,1)}, u32[]{:S(2)}) copy-start(bf16[512,512]{1,0:T(8,128)(2,1)} %table_ref.3) | copy-start | bytes 1572868
  11.3 3.9 %copy-start.2 = (f32[16,512]{1,0:T(8,128)S(1)}, f32[16,512]{1,0:T(8,128)}, u32[]{:S(2)}) copy-start(f32[16,512]{1,0:T(8,128)} %rates_ref.7) | copy-start | bytes 98308
  11.3 3.9 %copy-start.4 = (f32[512]{0:T(512)S(1)}, f32[512]{0:T(512)}, u32[]{:S(2)}) copy-start(f32[512]{0:T(512)} %param.13) | copy-start | bytes 6148
  11.3 2.7 %collective-permute-start = (s32[512]{0:T(512)S(1)}, s32[512]{0:T(512)S(1)}, u32[]{:S(2)}, u32[]{:S(2)}) collective-permute-start(s32[512]{0:T(512)S(1)} %copy-done.3), channel_id=1, source_target_pairs={{0,8},{8,16},{16,24},{24,32},{32,40},{40,48},{48,56},{56,64},{64,7... | collective-permute-start | bytes 6152 | tf_op jit(solution)/shard_map/ppermute | solution.py:542
  33.2 12.4 %copy-start.6 = (f32[16,512]{1,0:T(8,128)S(1)}, f32[16,512]{1,0:T(8,128)}, u32[]{:S(2)}) copy-start(f32[16,512]{1,0:T(8,128)} %residues_ref.1) | copy-start | bytes 98308
  33.9 16.8 %all-to-all-start.2 = ((bf16[8,16,512]{2,1,0:T(8,128)(2,1)}), bf16[8,16,512]{2,1,0:T(8,128)(2,1)S(1)}, u32[]{:S(2)}, u32[]{:S(2)}) async-start(bf16[8,16,512]{2,1,0:T(8,128)(2,1)} %get-tuple-element.14), calls=%async_computation.2 | async-start | bytes 262144 | tf_op jit(solution)/shard_map/all_to_all | solution.py:596

commit v5 on v4

--- a/solution.py
+++ b/solution.py
@@ -19,7 +19,7 @@
 EXT_STEPS = SPAN + HALO_STEPS + SPAN + STEPS
 OUT_STEPS = EXT_STEPS - SPAN
 HALO_IDS = 256
-BLOCK = 16
+BLOCK = 32
 SECOND_ROWS = (SPAN + STEPS) * LINES
 FREQS = 656
 INNER = 8

time: 53.2 us -> 53.1 us (level)
  no operation moved by 1% of the time
where the time goes in v5:
time: 53.1 us; the launch traced here: 52.8 us
  starting transfers between devices  22.2 us (42%)
  Pallas kernels  15.2 us (29%)
  blocking collectives  11.3 us (21%)
  waiting for transfers between devices  2.93 us (6%)
  local copies, waits for them, and re-layouts  1.1 us (2%)
    all_to_all x1, starting transfers between devices, local(): lax.all_to_all(totals, 'seq', 0, 0, axis_index_groups=far_groups, tiled=T...  11.6 us
    all_to_all x1, blocking collectives, local(): lax.all_to_all(state, 'seq', 0, 0, axis_index_groups=near_groups, tiled=T...  11.3 us
    all_to_all x1, starting transfers between devices, local(): squares = lax.all_to_all(partial, 'ch', 0, 0)  9.15 us
    pallas_call x1, Pallas kernels, local(): call(functools.partial(first_part, channels_of(width, shards)), 'first_pa...  6.72 us
    pallas_call x1, Pallas kernels, local(): call(second_part, 'second_part', [VMEM] * 4 + [FAR], [((count, width), BF...  4.09 us
    pallas_call x1, Pallas kernels, local(): call(functools.partial(third_part, inner), 'third_part', [SMEM] + [VMEM]...  2.12 us
    ppermute x1, starting transfers between devices, local(): lax.ppermute(token_ids, 'seq', [(i, i + 1) for i in range(length - 1)])  1.42 us
    all_to_all x1, waiting for transfers between devices, local(): squares = lax.all_to_all(partial, 'ch', 0, 0)  1.17 us
  transfers between devices with their start and end apart: 3, of which 3 were waited for; matrix products, arithmetic and copies ran while one was open for 0% of the time, Pallas kernels for 9%

profile of v5, /device:TPU:2, one launch (start us, length us, event | category | flops | bytes accessed | tf_op | source)
XLA Modules:
  0.0 52.8 jit_solution(12821905394537531229)
XLA Ops:
  0.0 0.0 copy-start
  0.0 1.0 %copy-done = bf16[512,512]{1,0:T(8,128)(2,1)S(1)} copy-done((bf16[512,512]{1,0:T(8,128)(2,1)S(1)}, bf16[512,512]{1,0:T(8,128)(2,1)}, u32[]{:S(2)}) %copy-start) | copy-done | bytes 524312
  1.0 0.0 copy-start.3
  1.0 0.0 copy-start.5
  1.0 0.0 copy-start.7
  1.0 1.0 %square_sums.1 = f32[8,1,512]{2,1,0:T(1,128)} custom-call(bf16[512,512]{1,0:T(8,128)(2,1)S(1)} %copy-done), custom_call_target="tpu_custom_call" | custom-call | flops 1000000000 | bytes 4000000 | tf_op jit(solution)/shard_map/square_sums/pallas_call | solution.py:543
  2.1 9.2 %all-to-all-start = ((f32[8,1,512]{2,1,0:T(1,128)}), f32[8,1,512]{2,1,0:T(1,128)S(1)}, u32[]{:S(2)}, u32[]{:S(2)}) async-start(f32[8,1,512]{2,1,0:T(1,128)} %square_sums.1), calls=%async_computation | async-start | bytes 32768 | tf_op jit(solution)/shard_map/all_to_all | solution.py:546
  11.2 0.0 copy-done.3
  11.2 0.0 copy-start.8
  11.2 0.0 copy-start.1
  11.3 0.0 copy-start.2
  11.3 0.0 copy-start.4
  11.3 1.4 %collective-permute-start = (s32[512]{0:T(512)S(1)}, s32[512]{0:T(512)S(1)}, u32[]{:S(2)}, u32[]{:S(2)}) collective-permute-start(s32[512]{0:T(512)S(1)} %copy-done.3), channel_id=1, source_target_pairs={{0,8},{8,16},{16,24},{24,32},{32,40},{40,48},{48,56},{56,64},{64,7... | collective-permute-start | bytes 6152 | tf_op jit(solution)/shard_map/ppermute | solution.py:542
  12.7 0.0 copy-done.5
  12.7 0.0 copy-done.7
  12.7 0.5 spectrum_of.1.spectrum_ref
  13.2 0.0 copy-done.8
  13.3 0.7 %collective-permute-done = s32[512]{0:T(512)S(1)} collective-permute-done((s32[512]{0:T(512)S(1)}, s32[512]{0:T(512)S(1)}, u32[]{:S(2)}, u32[]{:S(2)}) %collective-permute-start) | collective-permute-done | bytes 2080 | tf_op jit(solution)/shard_map/ppermute | solution.py:542
  14.0 1.2 %all-to-all-done.squares_ref = f32[8,1,512]{2,1,0:T(1,128)S(1)} async-done(((f32[8,1,512]{2,1,0:T(1,128)}), f32[8,1,512]{2,1,0:T(1,128)S(1)}, u32[]{:S(2)}, u32[]{:S(2)}) %all-to-all-start) | async-done | bytes 16416 | tf_op jit(solution)/shard_map/all_to_all | solution.py:546
  15.2 0.0 copy-done.1
  15.2 0.0 copy-done.2
  15.2 0.0 copy-done.4
  15.2 6.7 %first_part.1 = (bf16[8,16,512]{2,1,0:T(8,128)(2,1)S(1)}, bf16[1328,512]{1,0:T(8,128)(2,1)S(1)}) custom-call(s32[1]{0:T(128)} %bitcast.place_ref, f32[8,1,512]{2,1,0:T(1,128)S(1)} %all-to-all-done.squares_ref, s32[1,512]{1,0:T(1,128)S(1)} %bitcast.6, s32[1,512]{1,0:T(1,128)S(1)} %bitcast.4, bf16[512,512]{1,0:T(8,128)(2,1)S(1)} %copy-done.1, ...), custom_call_target="tpu_custom_call" | custom-call | flops 1000000000 | bytes 4000000 | tf_op jit(solution)/shard_map/first_part/pallas_call | solution.py:551
  21.9 11.3 %all_to_all.15.rows_ref = bf16[8,16,512]{2,1,0:T(8,128)(2,1)S(1)} all-to-all(bf16[8,16,512]{2,1,0:T(8,128)(2,1)S(1)} %get-tuple-element.12), channel_id=1, replica_groups={{40,24,48,16,56,8,0,32},{104,88,112,80,120,72,64,96},{168,152,176,144,1..., dimensions={0} | all-to-all | bytes 262144 | tf_op jit(solution)/shard_map/all_to_all | solution.py:578
  33.2 0.0 copy-start.6
  33.2 0.7 %near_part.1 = (f32[16,512]{1,0:T(8,128)S(1)}, bf16[8,16,512]{2,1,0:T(8,128)(2,1)}) custom-call(s32[1]{0:T(128)} %bitcast.place_ref, bf16[8,16,512]{2,1,0:T(8,128)(2,1)S(1)} %all_to_all.15.rows_ref, f32[16,512]{1,0:T(8,128)S(1)} %copy-done.2), custom_call_target="tpu_custom_call" | custom-call | flops 1000000000 | bytes 4000000 | tf_op jit(solution)/shard_map/near_part/pallas_call | solution.py:589
  33.9 11.6 %all-to-all-start.2 = ((bf16[8,16,512]{2,1,0:T(8,128)(2,1)}), bf16[8,16,512]{2,1,0:T(8,128)(2,1)S(1)}, u32[]{:S(2)}, u32[]{:S(2)}) async-start(bf16[8,16,512]{2,1,0:T(8,128)(2,1)} %get-tuple-element.14), calls=%async_computation.2 | async-start | bytes 262144 | tf_op jit(solution)/shard_map/all_to_all | solution.py:596
  45.5 0.0 copy-done.6
  45.5 4.1 %second_part.1 = (bf16[512,512]{1,0:T(8,128)(2,1)S(1)}, f32[512,512]{1,0:T(8,128)S(1)}, f32[16,512]{1,0:T(8,128)S(1)}) custom-call(f32[2,3,7,512]{3,2,1,0:T(8,128)S(1)} %copy.12.filters_ref, f32[16,512]{1,0:T(8,128)S(1)} %copy-done.2, f32[16,512]{1,0:T(8,128)S(1)} %copy-done.6, bf16[1328,512]{1,0:T(8,128)(2,1)S(1)} %get-tuple-element.15.kept_ref, ...), custom_call_target="tpu_custom_call" | custom-call | flops 4000000000 | bytes 10000000 | tf_op jit(solution)/shard_map/second_part/pallas_call | solution.py:579
  49.6 1.0 %all-to-all-done.2.totals_ref = bf16[8,16,512]{2,1,0:T(8,128)(2,1)S(1)} async-done(((bf16[8,16,512]{2,1,0:T(8,128)(2,1)}), bf16[8,16,512]{2,1,0:T(8,128)(2,1)S(1)}, u32[]{:S(2)}, u32[]{:S(2)}) %all-to-all-start.2) | async-done | bytes 131104 | tf_op jit(solution)/shard_map/all_to_all | solution.py:596
  50.7 2.1 %third_part.1 = bf16[512,512]{1,0:T(8,128)(2,1)} custom-call(s32[1]{0:T(128)} %bitcast.place_ref, f32[16,512]{1,0:T(8,128)S(1)} %get-tuple-element.13.near_ref, bf16[8,16,512]{2,1,0:T(8,128)(2,1)S(1)} %all-to-all-done.2.totals_ref, f32[16,512]{1,0:T(8,128)S(1)} %copy-done.2, f32[16,512]{1,0:T(8,128)S(1)} %get-tuple-element.16.weights_ref, ...), custom_call_target="tpu_custom_call" | custom-call | flops 1000000000 | bytes 4000000 | tf_op jit(solution)/shard_map/third_part/pallas_call | solution.py:597
  (1 shorter events, 0.0 us)
Async XLA Ops:
  0.0 1.0 %copy-start = (bf16[512,512]{1,0:T(8,128)(2,1)S(1)}, bf16[512,512]{1,0:T(8,128)(2,1)}, u32[]{:S(2)}) copy-start(bf16[512,512]{1,0:T(8,128)(2,1)} %table_ref.3) | copy-start | bytes 1572868
  1.0 10.2 %copy-start.3 = (s32[512]{0:T(512)S(1)}, s32[512]{0:T(512)}, u32[]{:S(2)}) copy-start(s32[512]{0:T(512)} %param.11) | copy-start | bytes 6148
  1.0 11.7 %copy-start.5 = (f32[128,512]{1,0:T(8,128)S(1)}, f32[128,512]{1,0:T(8,128)}, u32[]{:S(2)}) copy-start(f32[128,512]{1,0:T(8,128)} %medium_ref.1) | copy-start | bytes 786436
  1.0 11.7 %copy-start.7 = (bf16[656,384]{1,0:T(8,128)(2,1)S(1)}, bf16[656,384]{1,0:T(8,128)(2,1)}, u32[]{:S(2)}) copy-start(bf16[656,384]{1,0:T(8,128)(2,1)} %constant.14.clone.wave_ref) | copy-start | bytes 1511428
  2.1 13.1 %all-to-all-start = ((f32[8,1,512]{2,1,0:T(1,128)}), f32[8,1,512]{2,1,0:T(1,128)S(1)}, u32[]{:S(2)}, u32[]{:S(2)}) async-start(f32[8,1,512]{2,1,0:T(1,128)} %square_sums.1), calls=%async_computation | async-start | bytes 32768 | tf_op jit(solution)/shard_map/all_to_all | solution.py:546
  11.2 2.0 %copy-start.8 = (f32[2,3,7,512]{3,0,2,1:T(2,128)S(1)}, f32[2,3,7,512]{3,0,2,1:T(2,128)}, u32[]{:S(2)}) copy-start(f32[2,3,7,512]{3,0,2,1:T(2,128)} %param.14) | copy-start | bytes 258052
  11.2 3.9 %copy-start.1 = (bf16[512,512]{1,0:T(8,128)(2,1)S(1)}, bf16[512,512]{1,0:T(8,128)(2,1)}, u32[]{:S(2)}) copy-start(bf16[512,512]{1,0:T(8,128)(2,1)} %table_ref.3) | copy-start | bytes 1572868
  11.3 3.9 %copy-start.2 = (f32[16,512]{1,0:T(8,128)S(1)}, f32[16,512]{1,0:T(8,128)}, u32[]{:S(2)}) copy-start(f32[16,512]{1,0:T(8,128)} %rates_ref.7) | copy-start | bytes 98308
  11.3 3.9 %copy-start.4 = (f32[512]{0:T(512)S(1)}, f32[512]{0:T(512)}, u32[]{:S(2)}) copy-start(f32[512]{0:T(512)} %param.13) | copy-start | bytes 6148
  11.3 2.7 %collective-permute-start = (s32[512]{0:T(512)S(1)}, s32[512]{0:T(512)S(1)}, u32[]{:S(2)}, u32[]{:S(2)}) collective-permute-start(s32[512]{0:T(512)S(1)} %copy-done.3), channel_id=1, source_target_pairs={{0,8},{8,16},{16,24},{24,32},{32,40},{40,48},{48,56},{56,64},{64,7... | collective-permute-start | bytes 6152 | tf_op jit(solution)/shard_map/ppermute | solution.py:542
  33.2 12.4 %copy-start.6 = (f32[16,512]{1,0:T(8,128)S(1)}, f32[16,512]{1,0:T(8,128)}, u32[]{:S(2)}) copy-start(f32[16,512]{1,0:T(8,128)} %residues_ref.1) | copy-start | bytes 98308
  33.9 16.8 %all-to-all-start.2 = ((bf16[8,16,512]{2,1,0:T(8,128)(2,1)}), bf16[8,16,512]{2,1,0:T(8,128)(2,1)S(1)}, u32[]{:S(2)}, u32[]{:S(2)}) async-start(bf16[8,16,512]{2,1,0:T(8,128)(2,1)} %get-tuple-element.14), calls=%async_computation.2 | async-start | bytes 262144 | tf_op jit(solution)/shard_map/all_to_all | solution.py:596
